TPU v7x, 256 devices: a whole 4x4x8 slice. The times are simulated.
256 devices in a mesh: tensor: 2 (over x_hi), shard: 16 (over z, x_lo), replica: 8 (over y, core).
Axes of the slice: x: 4 (x_hi: 2, x_lo: 2; x = x_hi * 2 + x_lo), y: 4, z: 8, core: 2. Of those that a mesh axis runs over, the one named last changes fastest.
Arguments:
- activations: bfloat16 [32768, 16384], P(('shard', 'replica'), 'tensor'), may hold values from -24 to 24
- value_cotangent: bfloat16 [32768, 512], P(('shard', 'replica')), may hold values from -0.03125 to 0.03125
- key_gradient: float32 [16384, 512], P('shard', 'tensor'), may hold values from -6 to 6
- key_master: float32 [16384, 512], P('shard', 'tensor'), may hold values from -6 to 6
- key_moment: float32 [16384, 512], P('shard', 'tensor'), may hold values from -6 to 6
- key_second: float32 [16384, 512], P('shard', 'tensor'), may hold values from 0.01 to 1
- step_count: int32 [1], replicated, may hold values from 1 to 9
- previous_value: bfloat16 [16384, 512], P(('tensor', 'shard')), may hold values from -0.25 to 0.25
- previous_cotangent: bfloat16 [32768, 512], P(('shard', 'replica'), 'tensor'), may hold values from -6 to 6
Outputs:
- value_grad: float32 [16384, 512], P(('tensor', 'shard'))
- moment_new: float32 [16384, 512], P('shard', 'tensor')
- second_new: float32 [16384, 512], P('shard', 'tensor')
- key_update: float32 [16384, 512], P('shard', 'tensor')
- input_grad: bfloat16 [32768, 16384], P(('shard', 'replica'), 'tensor')
All inputs are finite; a program needn't handle non-finite values.
Results may differ from a plain program's by a relative error of at most 0.001.
Values may be sent and summed in bfloat16 or wider, within the bound.
A program may use at most 192 MiB of HBM per device.

v0:
```python
import jax
import jax.numpy as jnp
from jax import lax
from jax.sharding import PartitionSpec as P


def local(
    activations,
    value_cotangent,
    key_gradient,
    key_master,
    key_moment,
    key_second,
    step_count,
    previous_value,
    previous_cotangent,
):
    own_rows = lax.psum_scatter(
        lax.dot_general(
            activations,
            value_cotangent,
            (((0,), (0,)), ((), ())),
            preferred_element_type=jnp.float32,
        ),
        "shard",
        scatter_dimension=0,
        tiled=True,
    )
    value_grad = lax.psum(own_rows, "replica")
    moment_new = 0.9 * key_moment + 0.1 * key_gradient
    second_new = 0.95 * key_second + 0.05 * key_gradient * key_gradient
    steps_done = step_count.astype(jnp.float32)[0]
    first_fix = 1.0 - jnp.power(jnp.float32(0.9), steps_done)
    second_fix = 1.0 - jnp.power(jnp.float32(0.95), steps_done)
    key_update = (
        moment_new / first_fix / (jnp.sqrt(second_new / second_fix) + 1e-08) + 0.1 * key_master
    )
    whole_cotangent = lax.all_gather(previous_cotangent, "tensor", axis=1, tiled=True)
    input_grad = lax.dot_general(
        whole_cotangent,
        lax.all_gather(previous_value, "shard", axis=0, tiled=True),
        (((1,), (1,)), ((), ())),
        preferred_element_type=jnp.float32,
    ).astype(jnp.bfloat16)
    return (value_grad, moment_new, second_new, key_update, input_grad)


def solution(mesh):
    in_specs = (
        P(("shard", "replica"), "tensor"),
        P(("shard", "replica"), None),
        P("shard", "tensor"),
        P("shard", "tensor"),
        P("shard", "tensor"),
        P("shard", "tensor"),
        P(),
        P(("tensor", "shard"), None),
        P(("shard", "replica"), "tensor"),
    )
    out_specs = (
        P(("tensor", "shard"), None),
        P("shard", "tensor"),
        P("shard", "tensor"),
        P("shard", "tensor"),
        P(("shard", "replica"), "tensor"),
    )
    return jax.shard_map(local, mesh=mesh, in_specs=in_specs, out_specs=out_specs, check_vma=False)
```

profile of v0, /device:TPU:1, one launch (start us, length us, event | category | flops | bytes accessed | tf_op | source)
XLA Modules:
  0.0 637.0 jit_solution(7682991035550426488)
XLA Ops:
  7.2 0.0 copy-start
  7.2 0.0 reduce-scatter.2.cloned.1.call-start
  7.2 0.9 copy-done
  8.1 10.3 %fusion.2 = f32[8192,512]{1,0:T(8,128)} fusion(bf16[256,8192]{1,0:T(8,128)(2,1)} %param.9, bf16[256,512]{1,0:T(8,128)(2,1)S(1)} %copy-done), kind=kOutput, calls=%fused_computation.5 | convolution fusion | flops 2147483648 | bytes 21233664 | tf_op jit(solution)/shard_map/dot_general | solution.py:19
  18.4 0.0 copy-start.4
  18.4 0.0 copy-start.1
  18.4 0.0 copy-start.2
  18.4 0.0 copy-start.3
  18.4 0.0 reduce-scatter.2.cloned.1.call-update
  18.5 0.0 all-gather.2.cloned.1.call-start
  18.5 0.7 all-gather.2.cloned.1.call-update
  19.2 0.0 all-reduce.2.cloned.1.call-start
  20.2 0.0 copy-done.4
  20.2 6.7 %all_gather.6 = bf16[256,512]{1,0:T(8,128)(2,1)} all-gather(bf16[256,256]{1,0:T(8,128)(2,1)S(1)} %copy-done.4), channel_id=1, replica_groups=mesh['tensor'=2,'shard'=16,'replica'=8] {'tensor'}, dimensions={1}, use_global_device_ids=true | all-gather | bytes 393216 | tf_op jit(solution)/shard_map/all_gather | solution.py:38
  26.9 0.0 copy-done.1
  26.9 0.0 copy-done.2
  26.9 0.0 copy-done.3
  26.9 3.3 multiply_add_fusion
  30.2 343.8 %reduce-scatter.2.cloned.1.call-done = f32[512,512]{1,0:T(8,128)} async-done(((f32[8192,512]{1,0:T(8,128)}), f32[512,512]{1,0:T(8,128)}) %reduce-scatter.2.cloned.1.call-update) | async-done | bytes 1048592 | tf_op jit(solution)/shard_map/reduce_scatter | solution.py:18
  373.9 0.0 all-reduce.2.cloned.1.call-update
  374.0 185.1 %all-gather.2.cloned.1.call-done = bf16[8192,512]{1,0:T(8,128)(2,1)} async-done(((bf16[512,512]{1,0:T(8,128)(2,1)}), bf16[8192,512]{1,0:T(8,128)(2,1)}) %all-gather.2.cloned.1.call-update) | async-done | bytes 8388624 | tf_op jit(solution)/shard_map/all_gather | solution.py:41
  559.0 7.9 %convolution_convert_fusion = bf16[256,8192]{1,0:T(8,128)(2,1)} fusion(bf16[256,512]{1,0:T(8,128)(2,1)} %all_gather.6, bf16[8192,512]{1,0:T(8,128)(2,1)} %all-gather.2.cloned.1.call-done), kind=kOutput, calls=%fused_computation | convolution fusion | flops 2149580800 | bytes 12845056 | tf_op jit(solution)/shard_map/dot_general | solution.py:39
  566.9 61.3 %all-reduce.2.cloned.1.call-done = f32[512,512]{1,0:T(8,128)} async-done(((f32[512,512]{1,0:T(8,128)}), f32[512,512]{1,0:T(8,128)}) %all-reduce.2.cloned.1.call-update) | async-done | bytes 1048592 | tf_op jit(solution)/shard_map/psum | solution.py:29
  628.3 2.3 copy.16
Async XLA Ops:
  7.2 1.0 copy-start
  7.2 366.8 %reduce-scatter.2.cloned.1.call-start = ((), (), s32[]{:S(2)}) async-start(), calls=%async_computation.1 | async-start | bytes 17825792 | tf_op jit(solution)/shard_map/reduce_scatter | solution.py:18
  18.4 1.7 copy-start.4
  18.4 8.4 %copy-start.1 = (f32[1024,256]{1,0:T(8,128)S(1)}, f32[1024,256]{1,0:T(8,128)}, u32[]{:S(2)}) copy-start(f32[1024,256]{1,0:T(8,128)} %param.12) | copy-start | bytes 3145732
  18.4 8.4 %copy-start.2 = (f32[1024,256]{1,0:T(8,128)S(1)}, f32[1024,256]{1,0:T(8,128)}, u32[]{:S(2)}) copy-start(f32[1024,256]{1,0:T(8,128)} %param.11) | copy-start | bytes 3145732
  18.4 8.4 %copy-start.3 = (f32[1024,256]{1,0:T(8,128)S(1)}, f32[1024,256]{1,0:T(8,128)}, u32[]{:S(2)}) copy-start(f32[1024,256]{1,0:T(8,128)} %param.14) | copy-start | bytes 3145732
  18.5 540.6 %all-gather.2.cloned.1.call-start = ((), (), s32[]{:S(2)}) async-start(), calls=%async_computation.3 | async-start | bytes 8912896 | tf_op jit(solution)/shard_map/all_gather | solution.py:41
  19.2 609.0 %all-reduce.2.cloned.1.call-start = ((), (), s32[]{:S(2)}) async-start(), calls=%async_computation.2 | async-start | bytes 2097152 | tf_op jit(solution)/shard_map/psum | solution.py:29
Sparse Core Ops, SparseCore 0:
  18.6 355.3 reduce-scatter.1
  375.7 183.2 all-gather.1
  561.4 66.8 all-reduce.1
where the time goes:
time: 638 us; the launch traced here: 637 us
  waiting for transfers between devices  591 us (93%)
  matrix products  18.2 us (3%)
  between operations  14.7 us (2%)
  blocking collectives  6.69 us (1%)
    reduce_scatter x1, waiting for transfers between devices, local(): lax.psum_scatter(lax.dot_general(activations, value_cotangent, (((0,), (0...  344 us
    all_gather x1, waiting for transfers between devices, local(): lax.all_gather(previous_value, 'shard', axis=0, tiled=True)  185 us
    psum x1, waiting for transfers between devices, local(): value_grad = lax.psum(own_rows, 'replica')  61.3 us
  transfers between devices with their start and end apart: 3, of which 3 were waited for; matrix products, arithmetic and copies ran while one was open for 2% of the time, Pallas kernels for 0%

commit v1 on v0

v1 whole, which is shorter than its diff:
```python
import functools

import jax
import jax.numpy as jnp
from jax import lax
from jax.experimental import pallas as pl
from jax.experimental.pallas import tpu as pltpu
from jax.sharding import PartitionSpec as P

MESH = pl.DeviceIdType.MESH
F32, BF16, I16, I32 = jnp.float32, jnp.bfloat16, jnp.int16, jnp.int32
Z, Y = 8, 4
TOK, FEAT, COLS = 256, 8192, 512
HALF = 256
QUARTER = COLS // Y
STEPS = 12
HOPS = {1: (4, 3, 4), -1: (3, 4, 3)}


def coded(x):
    top = jnp.maximum(jnp.max(jnp.abs(x), axis=0, keepdims=True), 1e-30)
    return jnp.round(x * (32767.0 / top)).astype(I32).astype(I16), top * (1.0 / 32767.0)


def plain(q, scale):
    return q.astype(I32).astype(F32) * scale


def exchange(
    acts, g, pv, pc,
    w, cot, fin, fin_scale,
    a_own, a_par, g_buf, g_t, part,
    m1s, m1r, m1ss, m1sr, m2s, m2r, m2ss, m2sr,
    xs, xr, xss, xsr, zs, zr, zss, zsr,
    a_local, a_send, a_recv, one, w_recv, w_pair_recv, w_ring_send, w_x_send, w_pair_send,
    m1_send, m1_recv, m2_send, m2_recv, x_send, x_recv, z_send, z_recv, f_send, f_recv, fp_send, fp_recv,
):
    tensor = lax.axis_index("tensor")
    shard = lax.axis_index("shard")
    replica = lax.axis_index("replica")
    z, x = shard // 2, shard % 2
    y, core = replica // 2, replica % 2
    sgn = 1 - 2 * core

    def ring(at, n):
        return lax.rem(at + 2 * n, n)

    to_pair = (tensor, shard, y * 2 + 1 - core)
    to_x = (tensor, z * 2 + 1 - x, replica)
    to_tensor = (1 - tensor, shard, replica)

    def to_y(r):
        return (tensor, shard, ring(y + r, Y) * 2 + core)

    def to_z(way):
        return (tensor, ring(z + way * sgn, Z) * 2 + x, replica)

    def remote(src, dst, send, recv, device):
        return pltpu.make_async_remote_copy(
            src_ref=src, dst_ref=dst, send_sem=send, recv_sem=recv, device_id=device, device_id_type=MESH
        )

    barrier = pltpu.get_barrier_semaphore()
    peers = (to_pair, to_x, to_tensor, to_y(1), to_y(2), to_y(3), to_z(1), to_z(-1))
    for peer in peers:
        pl.semaphore_signal(barrier, inc=1, device_id=peer, device_id_type=MESH)
    pl.semaphore_wait(barrier, len(peers))

    def columns(t, b, of_core):
        far = Z // 2 - (t + 1) // 2
        offset = jnp.where(t % 2 == 1, far, -far) * (1 - 2 * of_core)
        start = (ring(z + offset, Z) * 2 + b) * 2 * HALF + of_core * HALF
        return pl.ds(pl.multiple_of(start, HALF), HALF)

    def own_acts(t, b):
        return pltpu.make_async_copy(
            acts.at[:, columns(t, b, core)], a_own.at[t, :, pl.ds(b * HALF, HALF)], a_local.at[t, b]
        )

    def pair_acts(t, b):
        return remote(
            acts.at[:, columns(t, b, 1 - core)], a_par.at[t, :, pl.ds(b * HALF, HALF)],
            a_send.at[t, b], a_recv.at[t, b], to_pair,
        )

    own_g = pltpu.make_async_copy(g, g_buf.at[0], one.at[0])
    pair_g = remote(g, g_buf.at[1], one.at[1], one.at[2], to_pair)
    own_w = pltpu.make_async_copy(pv, w.at[pl.ds(pl.multiple_of(shard * 4, 4), 4)], one.at[3])
    own_cot = pltpu.make_async_copy(pc, cot.at[:, pl.ds(pl.multiple_of(tensor * 256, 256), 256)], one.at[4])
    pair_cot = remote(pc, cot.at[:, pl.ds(pl.multiple_of(tensor * 256, 256), 256)], one.at[5], one.at[6], to_tensor)

    def slot(zo, xo, half, of_core):
        return ((zo * 2 + xo) * 2 + of_core) * 2 + half

    def mark(zo, xo, half):
        return (zo * 2 + xo) * 2 + half

    def flow_of(flow):
        return (1 - x if flow == 1 else x), (1 if flow == 2 else 0)

    def origin(way, k):
        return ring(z - way * sgn * k, Z)

    def ring_copy(flow, way, k):
        xo, half = flow_of(flow)
        zo = origin(way, k)
        at = w.at[slot(zo, xo, half, core)]
        return remote(at, at, w_ring_send.at[0 if way == 1 else 1, flow * 4 + k], w_recv.at[mark(zo, xo, half)], to_z(way))

    def x_copy(zo, half, k):
        at = w.at[slot(zo, x, half, core)]
        return remote(at, at, w_x_send.at[k], w_recv.at[mark(zo, x, half)], to_x)

    def pair_copy(zo, xo, half):
        at = w.at[slot(zo, xo, half, core)]
        return remote(at, at, w_pair_send.at[mark(zo, xo, half)], w_pair_recv.at[mark(zo, xo, half)], to_pair)

    def arrive(zo, xo, half):
        at = w.at[slot(zo, xo, half, core)]
        remote(at, at, w_x_send.at[0], w_recv.at[mark(zo, xo, half)], to_x).wait_recv()

    def x_index(way, k):
        return 2 * k + (0 if way == 1 else 1)

    def ring_event(flow, way, k):
        xo, half = flow_of(flow)
        zo = origin(way, k)
        arrive(zo, xo, half)

        @pl.when(k < HOPS[way][flow])
        def _():
            ring_copy(flow, way, k).start()

        if flow == 2:
            x_copy(zo, half, x_index(way, k)).start()
        pair_copy(zo, xo, half).start()

    def x_event(way, k):
        zo = origin(way, k)
        arrive(zo, 1 - x, 1)
        pair_copy(zo, 1 - x, 1).start()

    own_g.start()
    pair_g.start()
    own_w.start()

    def start_acts(t, carry):
        for b in range(2):
            own_acts(t, b).start()
            pair_acts(t, b).start()
        return carry

    lax.fori_loop(0, 1, start_acts, 0)
    own_w.wait()
    x_copy(z, 0, 0).start()
    for way in (1, -1):
        ring_copy(0, way, 0).start()
    x_copy(z, 1, 1).start()
    for way in (1, -1):
        ring_copy(2, way, 0).start()
    lax.fori_loop(1, Z, start_acts, 0)
    own_cot.start()
    pair_cot.start()

    own_g.wait()
    pair_g.wait_recv()
    for r in range(Y):
        take = pl.ds(pl.multiple_of(ring(y + r, Y) * QUARTER, QUARTER), QUARTER)
        for b in range(2):
            g_t[r * QUARTER : (r + 1) * QUARTER, b * TOK : (b + 1) * TOK] = (
                g_buf[b, :, take].astype(F32).T.astype(BF16)
            )

    A, B = slice(0, QUARTER // 2), slice(QUARTER // 2, QUARTER)
    half_rows = QUARTER // 2

    def rows(r, first=0, count=QUARTER):
        return pl.ds(r * QUARTER + first, count)

    def along_y(src, dst, src_scale, dst_scale, send, recv, t, way):
        to = to_y(1 if way == 0 else 3)
        return (
            remote(src.at[t, way], dst.at[t, way], send.at[t, way, 0], recv.at[t, way, 0], to),
            remote(src_scale.at[t, way], dst_scale.at[t, way], send.at[t, way, 1], recv.at[t, way, 1], to),
        )

    m1 = functools.partial(along_y, m1s, m1r, m1ss, m1sr, m1_send, m1_recv)
    m2 = functools.partial(along_y, m2s, m2r, m2ss, m2sr, m2_send, m2_recv)

    def across_x(t):
        return (
            remote(xs.at[t], xr.at[t], x_send.at[t, 0], x_recv.at[t, 0], to_x),
            remote(xss.at[t], xsr.at[t], x_send.at[t, 1], x_recv.at[t, 1], to_x),
        )

    def along_z(j, way, first=0, count=QUARTER):
        part_of = pl.ds(first, count)
        return (
            remote(zs.at[j, part_of], zr.at[j, part_of], z_send.at[j, 0], z_recv.at[j, 0], to_z(way)),
            remote(zss.at[j], zsr.at[j], z_send.at[j, 1], z_recv.at[j, 1], to_z(way)),
        )

    def start(copies):
        for copy in copies:
            copy.start()

    def wait_recv(copies):
        for copy in copies:
            copy.wait_recv()

    def wait_send(copies):
        for copy in copies:
            copy.wait_send()

    def multiply(t):
        for b in range(2):
            own_acts(t, b).wait()
        part[t] = jnp.dot(g_t[:, :TOK], a_own[t], preferred_element_type=F32)
        for b in range(2):
            pair_acts(t, b).wait_recv()
        part[t] += jnp.dot(g_t[:, TOK:], a_par[t], preferred_element_type=F32)
        up = jnp.concatenate([part[t, rows(2, 0, half_rows)], part[t, rows(1, half_rows, half_rows)]], axis=0)
        m1s[t, 0], m1ss[t, 0] = coded(up)
        start(m1(t, 0))
        down = jnp.concatenate([part[t, rows(2, half_rows, half_rows)], part[t, rows(3, 0, half_rows)]], axis=0)
        m1s[t, 1], m1ss[t, 1] = coded(down)
        start(m1(t, 1))

    def combine(t):
        wait_recv(m1(t, 0))
        got = plain(m1r[t, 0], m1sr[t, 0])
        m2s[t, 0], m2ss[t, 0] = coded(part[t, rows(1, 0, half_rows)] + got[A])
        start(m2(t, 0))
        part[t, rows(0, half_rows, half_rows)] += got[B]
        wait_recv(m1(t, 1))
        got = plain(m1r[t, 1], m1sr[t, 1])
        m2s[t, 1], m2ss[t, 1] = coded(part[t, rows(3, half_rows, half_rows)] + got[A])
        start(m2(t, 1))
        part[t, rows(0, 0, half_rows)] += got[B]

    def cross(t):
        wait_recv(m2(t, 0))
        part[t, rows(0, 0, half_rows)] += plain(m2r[t, 0], m2sr[t, 0])
        wait_recv(m2(t, 1))
        part[t, rows(0, half_rows, half_rows)] += plain(m2r[t, 1], m2sr[t, 1])
        xs[t], xss[t] = coded(part[t, rows(0), pl.ds(pl.multiple_of((1 - x) * HALF, HALF), HALF)])
        start(across_x(t))

    def crossed(t):
        wait_recv(across_x(t))
        return part[t, rows(0), pl.ds(pl.multiple_of(x * HALF, HALF), HALF)] + plain(xr[t], xsr[t])

    def travel(t):
        @pl.when(t == 0)
        def _():
            here = crossed(0)
            zs[0, A], zss[0] = coded(here[A])
            start(along_z(0, 1, 0, half_rows))
            zs[1, B], zss[1] = coded(here[B])
            start(along_z(1, -1, half_rows, half_rows))

        @pl.when(t == 1)
        def _():
            here = crossed(1)
            wait_recv(along_z(0, 1, 0, half_rows))
            zs[2], zss[2] = coded(jnp.concatenate([here[A] + plain(zr[0, A], zsr[0]), here[B]], axis=0))
            start(along_z(2, 1))

        @pl.when(t == 2)
        def _():
            here = crossed(2)
            wait_recv(along_z(1, -1, half_rows, half_rows))
            zs[3], zss[3] = coded(jnp.concatenate([here[A], here[B] + plain(zr[1, B], zsr[1])], axis=0))
            start(along_z(3, -1))

        for way in (1, -1):

            @pl.when((t >= 3) & (t <= 6) & (t % 2 == (1 if way == 1 else 0)))
            def _():
                here = crossed(t)
                wait_recv(along_z(t - 1, way))
                zs[t + 1], zss[t + 1] = coded(here + plain(zr[t - 1], zsr[t - 1]))
                start(along_z(t + 1, way))

        @pl.when(t == 7)
        def _():
            here = crossed(7)
            for way in (1, -1):
                j = 6 if way == 1 else 7
                wait_recv(along_z(j, way))
                here += plain(zr[j], zsr[j])
            fin[core * 4 + y], fin_scale[core * 4 + y] = coded(here)

    def weights(t):
        k = t // 2 + 1

        @pl.when(t == 0)
        def _():
            arrive(z, 1 - x, 0)
            for way in (1, -1):
                ring_copy(1, way, 0).start()
            pair_copy(z, 1 - x, 0).start()

        for flow, parity in ((0, 0), (2, 0), (1, 1)):
            for way in (1, -1):

                @pl.when((t % 2 == parity) & (k <= HOPS[way][flow]))
                def _():
                    ring_event(flow, way, k)

        @pl.when(t == 1)
        def _():
            x_event(1, 0)

        for way in (1, -1):

            @pl.when((t % 2 == 1) & (k >= 2))
            def _():
                x_event(way, k - 1)

    def step(t, carry):
        @pl.when(t < Z)
        def _():
            multiply(t)

        @pl.when((t >= 1) & (t <= Z))
        def _():
            weights(t - 1)

        @pl.when((t >= 2) & (t < Z + 2))
        def _():
            combine(t - 2)

        @pl.when((t >= 3) & (t < Z + 3))
        def _():
            cross(t - 3)

        @pl.when(t >= 4)
        def _():
            travel(t - 4)

        return carry

    lax.fori_loop(0, STEPS, step, 0)
    x_event(1, 4)

    def fin_copy(r, of, device, send, recv):
        at = of * 4 + ring(y - r, Y) if not isinstance(of, tuple) else of[0]
        return (
            remote(fin.at[at], fin.at[at], send.at[r, 0], recv.at[r, 0], device),
            remote(fin_scale.at[at], fin_scale.at[at], send.at[r, 1], recv.at[r, 1], device),
        )

    def to_replica(r):
        return fin_copy(r, (core * 4 + y,), to_y(r), f_send, f_recv)

    def to_partner(r):
        return fin_copy(r, core, to_pair, fp_send, fp_recv)

    for r in (2, 1, 3):
        start(to_replica(r))
    start(to_partner(0))
    for r in (1, 3, 2):
        wait_recv(fin_copy(r, core, to_y(r), f_send, f_recv))
        start(to_partner(r))
    for r in range(Y):
        wait_recv(fin_copy(r, 1 - core, to_pair, fp_send, fp_recv))

    own_cot.wait()
    pair_cot.wait_send()
    other = cot.at[:, pl.ds(pl.multiple_of((1 - tensor) * 256, 256), 256)]
    remote(pc, other, one.at[5], one.at[6], to_tensor).wait_recv()
    pair_g.wait_send()

    def finish(t, carry):
        for b in range(2):
            pair_acts(t, b).wait_send()
        for way in range(2):
            wait_send(m1(t, way))
            wait_send(m2(t, way))
        wait_send(across_x(t))
        return carry

    lax.fori_loop(0, Z, finish, 0)
    wait_send(along_z(0, 1, 0, half_rows))
    wait_send(along_z(1, -1, half_rows, half_rows))

    def finish_z(j, carry):
        wait_send(along_z(j, 1))
        return carry

    lax.fori_loop(2, Z, finish_z, 0)
    for r in range(Y):
        if r:
            wait_send(to_replica(r))
        wait_send(to_partner(r))
    for way in (1, -1):
        for flow in range(3):
            for k in range(HOPS[way][flow]):
                ring_copy(flow, way, k).wait_send()
    x_copy(z, 0, 0).wait_send()
    x_copy(z, 1, 1).wait_send()
    for way in (1, -1):
        for k in range(1, HOPS[way][2] + 1):
            x_copy(origin(way, k), 1, x_index(way, k)).wait_send()

    def finish_w(i, carry):
        zo, xo, half = i // 4, (i // 2) % 2, i % 2

        @pl.when(i // 2 != shard)
        def _():
            pair_copy(zo, xo, half).wait_send()
            at = w.at[slot(zo, xo, half, 1 - core)]
            remote(at, at, w_pair_send.at[i], w_pair_recv.at[i], to_pair).wait_recv()

        return carry

    lax.fori_loop(0, 4 * Z, finish_w, 0)


def gathered(acts, g, pv, pc):
    dma = pltpu.SemaphoreType.DMA
    any_, vmem = pl.BlockSpec(memory_space=pl.ANY), pl.BlockSpec(memory_space=pltpu.VMEM)
    S = jax.ShapeDtypeStruct
    return pl.pallas_call(
        exchange,
        out_shape=(S((64, 128, 512), BF16), S((256, 512), BF16), S((8, QUARTER, HALF), I16), S((8, 1, HALF), F32)),
        in_specs=[any_] * 4,
        out_specs=(vmem,) * 4,
        scratch_shapes=[
            pltpu.VMEM((Z, TOK, 2 * HALF), BF16),
            pltpu.VMEM((Z, TOK, 2 * HALF), BF16),
            pltpu.VMEM((2, TOK, COLS), BF16),
            pltpu.VMEM((COLS, 2 * TOK), BF16),
            pltpu.VMEM((Z, COLS, 2 * HALF), F32),
            *[pltpu.VMEM((Z, 2, QUARTER, 2 * HALF), I16)] * 2,
            *[pltpu.VMEM((Z, 2, 1, 2 * HALF), F32)] * 2,
            *[pltpu.VMEM((Z, 2, QUARTER // 2, 2 * HALF), I16)] * 2,
            *[pltpu.VMEM((Z, 2, 1, 2 * HALF), F32)] * 2,
            *[pltpu.VMEM((Z, QUARTER, HALF), I16)] * 2,
            *[pltpu.VMEM((Z, 1, HALF), F32)] * 2,
            *[pltpu.VMEM((Z, QUARTER, HALF), I16)] * 2,
            *[pltpu.VMEM((Z, 1, HALF), F32)] * 2,
            dma((Z, 2)), dma((Z, 2)), dma((Z, 2)), dma((7,)),
            dma((32,)), dma((32,)), dma((2, 12)), dma((10,)), dma((32,)),
            dma((Z, 2, 2)), dma((Z, 2, 2)), dma((Z, 2, 2)), dma((Z, 2, 2)),
            dma((Z, 2)), dma((Z, 2)), dma((Z, 2)), dma((Z, 2)),
            dma((Y, 2)), dma((Y, 2)), dma((Y, 2)), dma((Y, 2)),
        ],
        compiler_params=pltpu.CompilerParams(
            collective_id=1, has_side_effects=True, vmem_limit_bytes=48 << 20
        ),
    )(acts, g, pv.reshape(4, 128, 512), pc)


def local(
    activations,
    value_cotangent,
    key_gradient,
    key_master,
    key_moment,
    key_second,
    step_count,
    previous_value,
    previous_cotangent,
):
    weights, cotangent, fin, fin_scale = gathered(activations, value_cotangent, previous_value, previous_cotangent)
    blocks = (fin.astype(F32) * fin_scale).reshape(2, Y, QUARTER, HALF)
    value_grad = blocks.transpose(0, 3, 1, 2).reshape(2 * HALF, COLS)
    moment_new = 0.9 * key_moment + 0.1 * key_gradient
    second_new = 0.95 * key_second + 0.05 * key_gradient * key_gradient
    steps_done = step_count.astype(jnp.float32)[0]
    first_fix = 1.0 - jnp.power(jnp.float32(0.9), steps_done)
    second_fix = 1.0 - jnp.power(jnp.float32(0.95), steps_done)
    key_update = (
        moment_new / first_fix / (jnp.sqrt(second_new / second_fix) + 1e-08) + 0.1 * key_master
    )
    input_grad = lax.dot_general(
        cotangent,
        weights.reshape(FEAT, COLS),
        (((1,), (1,)), ((), ())),
        preferred_element_type=jnp.float32,
    ).astype(jnp.bfloat16)
    return (value_grad, moment_new, second_new, key_update, input_grad)


def solution(mesh):
    in_specs = (
        P(("shard", "replica"), "tensor"),
        P(("shard", "replica"), None),
        P("shard", "tensor"),
        P("shard", "tensor"),
        P("shard", "tensor"),
        P("shard", "tensor"),
        P(),
        P(("tensor", "shard"), None),
        P(("shard", "replica"), "tensor"),
    )
    out_specs = (
        P(("tensor", "shard"), None),
        P("shard", "tensor"),
        P("shard", "tensor"),
        P("shard", "tensor"),
        P(("shard", "replica"), "tensor"),
    )
    return jax.shard_map(local, mesh=mesh, in_specs=in_specs, out_specs=out_specs, check_vma=False)
```

time: 638 us -> 92.2 us (0.14)
  waiting for transfers between devices: 591 us -> 0 us
  Pallas kernels: 0 us -> 72.1 us
  between operations: 14.7 us -> 1.41 us
  matrix products: 18.2 us -> 7.86 us
  blocking collectives: 6.69 us -> 0 us
    reduce_scatter x1 -> x0, waiting for transfers between devices: 344 us -> none  [local(): lax.psum_scatter(lax.dot_general(activations, value_cotangent, (((0,), (0...]
    all_gather x1 -> x0, waiting for transfers between devices: 185 us -> none  [local(): lax.all_gather(previous_value, 'shard', axis=0, tiled=True)]
    pallas_call x0 -> x1, Pallas kernels: none -> 72.1 us  [gathered(): pl.pallas_call(exchange, out_shape=(S((64, 128, 512), BF16), S((256, 512)...]
    psum x1 -> x0, waiting for transfers between devices: 61.3 us -> none  [local(): value_grad = lax.psum(own_rows, 'replica')]
    dot_general x2 -> x1, matrix products: 18.2 us -> 7.86 us  [local(): lax.dot_general(cotangent, weights.reshape(FEAT, COLS), (((1,), (1,)), ((...]
    all_gather x1 -> x0, blocking collectives: 6.69 us -> none  [local(): lax.all_gather(previous_cotangent, 'tensor', axis=1, tiled=True)]
  transfers between devices with their start and end apart: 3 -> 0, of which waited for: 3 -> 0; matrix products, arithmetic and copies ran while one was open for 2% -> 0% of each run, Pallas kernels for 0% -> 0%
where the time goes in v1:
time: 92.2 us; the launch traced here: 91.9 us
  Pallas kernels  72.1 us (78%)
  matrix products  7.86 us (9%)
  local copies, waits for them, and re-layouts  6.5 us (7%)
  other arithmetic  4.1 us (4%)
  between operations  1.41 us (2%)
    pallas_call x1, Pallas kernels, gathered(): pl.pallas_call(exchange, out_shape=(S((64, 128, 512), BF16), S((256, 512)...  72.1 us
    dot_general x1, matrix products, local(): lax.dot_general(cotangent, weights.reshape(FEAT, COLS), (((1,), (1,)), ((...  7.86 us
    unnamed x12, local copies, waits for them, and re-layouts  6.12 us
    add x1, other arithmetic, local(): moment_new / first_fix / (jnp.sqrt(second_new / second_fix) + 1e-08)  3.92 us

profile of v1, /device:TPU:1, one launch (start us, length us, event | category | flops | bytes accessed | tf_op | source)
XLA Modules:
  0.0 91.9 jit_solution(17505786130309693964)
XLA Ops:
  0.6 0.0 copy-start
  0.6 2.2 %copy-done = bf16[256,8192]{1,0:T(8,128)(2,1)S(1)} copy-done((bf16[256,8192]{1,0:T(8,128)(2,1)S(1)}, bf16[256,8192]{1,0:T(8,128)(2,1)}, u32[]{:S(2)}) %copy-start) | copy-done | bytes 4194328
  2.8 0.0 copy-start.1
  2.8 1.0 %copy-done.1 = bf16[512,512]{1,0:T(8,128)(2,1)S(1)} copy-done((bf16[512,512]{1,0:T(8,128)(2,1)S(1)}, bf16[512,512]{1,0:T(8,128)(2,1)}, u32[]{:S(2)}) %copy-start.1) | copy-done | bytes 524312
  3.9 0.0 copy-start.2
  3.9 0.9 %copy-done.2 = bf16[256,512]{1,0:T(8,128)(2,1)S(1)} copy-done((bf16[256,512]{1,0:T(8,128)(2,1)S(1)}, bf16[256,512]{1,0:T(8,128)(2,1)}, u32[]{:S(2)}) %copy-start.2) | copy-done | bytes 262168
  4.8 0.0 copy-start.3
  4.8 0.9 copy-done.3
  5.7 72.1 %shard_map.128 = (bf16[64,128,512]{2,1,0:T(8,128)(2,1)}, bf16[256,512]{1,0:T(8,128)(2,1)S(1)}, s16[8,128,256]{2,1,0:T(8,128)(2,1)S(1)}, f32[8,1,256]{2,1,0:T(1,128)S(1)}) custom-call(bf16[256,8192]{1,0:T(8,128)(2,1)S(1)} %copy-done, bf16[256,512]{1,0:T(8,128)(2,1)S(1)} %copy-done.2, bf16[4,128,512]{2,1,0:T(8,128)(2,1)S(1)} %bitcast.17, ...), custom_call_target="tpu_custom_call" | custom-call | tf_op jit(solution)/shard_map/pallas_call | solution.py:425
  77.8 0.0 copy-start.4
  77.8 7.9 %convolution_convert_fusion = bf16[256,8192]{1,0:T(8,128)(2,1)} fusion(bf16[256,512]{1,0:T(8,128)(2,1)S(1)} %get-tuple-element.11, bf16[8192,512]{1,0:T(8,128)(2,1)} %bitcast.22), kind=kOutput, calls=%fused_computation | convolution fusion | flops 2149580800 | bytes 12845056 | tf_op jit(solution)/shard_map/dot_general | solution.py:478
  85.7 0.2 convert_multiply_fusion
  85.8 0.4 copy.14
  86.2 1.0 %copy.19 = f32[64,8,4,128]{3,1,2,0:T(8,128)} copy(f32[64,8,4,128]{3,2,1,0:T(4,128)S(1)} %bitcast.19) | data formatting | bytes 2097152
  88.0 0.0 copy-done.4
  88.0 3.9 %multiply_add_fusion = (f32[1024,256]{1,0:T(8,128)}, f32[1024,256]{1,0:T(8,128)}, f32[1024,256]{1,0:T(8,128)}) fusion(f32[1024,256]{1,0:T(8,128)S(1)} %copy-done.4, f32[]{:T(128)} %bitcast.4, f32[]{:T(128)} %bitcast.3, f32[1024,256]{1,0:T(8,128)} %param.11, f32[1024,256]{1,0:T(8,128)} %param.14, f32[1024,256]{1,0:T(8,128)} %param.13), kind=kLoop, calls=%fused_computation.4 | loop fusion | flops 3407872 | bytes 7340040 | tf_op jit(solution)/shard_map/add | solution.py:476
  (1 shorter events, 0.0 us)
Async XLA Ops:
  0.6 2.2 %copy-start = (bf16[256,8192]{1,0:T(8,128)(2,1)S(1)}, bf16[256,8192]{1,0:T(8,128)(2,1)}, u32[]{:S(2)}) copy-start(bf16[256,8192]{1,0:T(8,128)(2,1)} %acts.1) | copy-start | bytes 12582916
  2.8 1.0 %copy-start.1 = (bf16[512,512]{1,0:T(8,128)(2,1)S(1)}, bf16[512,512]{1,0:T(8,128)(2,1)}, u32[]{:S(2)}) copy-start(bf16[512,512]{1,0:T(8,128)(2,1)} %param.16) | copy-start | bytes 1572868
  3.9 0.9 %copy-start.2 = (bf16[256,512]{1,0:T(8,128)(2,1)S(1)}, bf16[256,512]{1,0:T(8,128)(2,1)}, u32[]{:S(2)}) copy-start(bf16[256,512]{1,0:T(8,128)(2,1)} %g.1) | copy-start | bytes 786436
  4.8 0.9 copy-start.3
  77.8 10.2 %copy-start.4 = (f32[1024,256]{1,0:T(8,128)S(1)}, f32[1024,256]{1,0:T(8,128)}, u32[]{:S(2)}) copy-start(f32[1024,256]{1,0:T(8,128)} %param.12) | copy-start | bytes 3145732

commit v2 on v1

--- a/solution.py
+++ b/solution.py
@@ -1,4 +1,5 @@
 import functools
+import math
 
 import jax
 import jax.numpy as jnp
@@ -13,7 +14,10 @@
 TOK, FEAT, COLS = 256, 8192, 512
 HALF = 256
 QUARTER = COLS // Y
-STEPS = 12
+AHEAD = 3
+CROSS_LAG, TRAVEL_LAG = 3, 5
+SPLIT = 160
+LOG_KEEP_FIRST, LOG_KEEP_SECOND = math.log(0.9), math.log(0.95)
 HOPS = {1: (4, 3, 4), -1: (3, 4, 3)}
 
 
@@ -27,12 +31,12 @@
 
 
 def exchange(
-    acts, g, pv, pc,
-    w, cot, fin, fin_scale,
-    a_own, a_par, g_buf, g_t, part,
+    steps, acts, g, pv, pc, key_in,
+    input_grad, key_out, fin, fin_scale,
+    w, cot, key_buf, a_own, a_par, g_buf, g_t, part,
     m1s, m1r, m1ss, m1sr, m2s, m2r, m2ss, m2sr,
     xs, xr, xss, xsr, zs, zr, zss, zsr,
-    a_local, a_send, a_recv, one, w_recv, w_pair_recv, w_ring_send, w_x_send, w_pair_send,
+    key_sem, a_local, a_send, a_recv, one, w_recv, w_pair_recv, w_ring_send, w_x_send, w_pair_send,
     m1_send, m1_recv, m2_send, m2_recv, x_send, x_recv, z_send, z_recv, f_send, f_recv, fp_send, fp_recv,
 ):
     tensor = lax.axis_index("tensor")
@@ -64,7 +68,6 @@
     peers = (to_pair, to_x, to_tensor, to_y(1), to_y(2), to_y(3), to_z(1), to_z(-1))
     for peer in peers:
         pl.semaphore_signal(barrier, inc=1, device_id=peer, device_id_type=MESH)
-    pl.semaphore_wait(barrier, len(peers))
 
     def columns(t, b, of_core):
         far = Z // 2 - (t + 1) // 2
@@ -85,12 +88,13 @@
 
     own_g = pltpu.make_async_copy(g, g_buf.at[0], one.at[0])
     pair_g = remote(g, g_buf.at[1], one.at[1], one.at[2], to_pair)
-    own_w = pltpu.make_async_copy(pv, w.at[pl.ds(pl.multiple_of(shard * 4, 4), 4)], one.at[3])
+    own_w = pltpu.make_async_copy(pv, w.at[shard], one.at[3])
     own_cot = pltpu.make_async_copy(pc, cot.at[:, pl.ds(pl.multiple_of(tensor * 256, 256), 256)], one.at[4])
     pair_cot = remote(pc, cot.at[:, pl.ds(pl.multiple_of(tensor * 256, 256), 256)], one.at[5], one.at[6], to_tensor)
 
-    def slot(zo, xo, half, of_core):
-        return ((zo * 2 + xo) * 2 + of_core) * 2 + half
+    def block(zo, xo, half, of_core):
+        first, count = ((0, SPLIT), (SPLIT, HALF - SPLIT))[half]
+        return w.at[zo * 2 + xo, pl.ds(pl.multiple_of(of_core * HALF + first, 16), count)]
 
     def mark(zo, xo, half):
         return (zo * 2 + xo) * 2 + half
@@ -104,19 +108,19 @@
     def ring_copy(flow, way, k):
         xo, half = flow_of(flow)
         zo = origin(way, k)
-        at = w.at[slot(zo, xo, half, core)]
+        at = block(zo, xo, half, core)
         return remote(at, at, w_ring_send.at[0 if way == 1 else 1, flow * 4 + k], w_recv.at[mark(zo, xo, half)], to_z(way))
 
     def x_copy(zo, half, k):
-        at = w.at[slot(zo, x, half, core)]
+        at = block(zo, x, half, core)
         return remote(at, at, w_x_send.at[k], w_recv.at[mark(zo, x, half)], to_x)
 
     def pair_copy(zo, xo, half):
-        at = w.at[slot(zo, xo, half, core)]
+        at = block(zo, xo, half, core)
         return remote(at, at, w_pair_send.at[mark(zo, xo, half)], w_pair_recv.at[mark(zo, xo, half)], to_pair)
 
     def arrive(zo, xo, half):
-        at = w.at[slot(zo, xo, half, core)]
+        at = block(zo, xo, half, core)
         remote(at, at, w_x_send.at[0], w_recv.at[mark(zo, xo, half)], to_x).wait_recv()
 
     def x_index(way, k):
@@ -140,36 +144,49 @@
         arrive(zo, 1 - x, 1)
         pair_copy(zo, 1 - x, 1).start()
 
-    own_g.start()
-    pair_g.start()
-    own_w.start()
-
-    def start_acts(t, carry):
+    def key_copy(i):
+        return pltpu.make_async_copy(key_in[i], key_buf.at[i], key_sem.at[i])
+
+    def turned_g(b):
+        for r in range(Y):
+            take = pl.ds(pl.multiple_of(ring(y + r, Y) * QUARTER, QUARTER), QUARTER)
+            g_t[r * QUARTER : (r + 1) * QUARTER, b * TOK : (b + 1) * TOK] = (
+                g_buf[b, :, take].astype(F32).T.astype(BF16)
+            )
+
+    def start_own(t, carry):
         for b in range(2):
             own_acts(t, b).start()
+        return carry
+
+    def start_pair(t, carry):
+        for b in range(2):
             pair_acts(t, b).start()
         return carry
 
-    lax.fori_loop(0, 1, start_acts, 0)
+    own_g.start()
+    own_w.start()
+    lax.fori_loop(0, Z, start_own, 0)
+    own_cot.start()
+    for i in range(4):
+        key_copy(i).start()
+    own_g.wait()
+    turned_g(0)
     own_w.wait()
+    pl.semaphore_wait(barrier, len(peers))
+
+    pair_g.start()
+    lax.fori_loop(0, 1, start_pair, 0)
+    pair_cot.start()
     x_copy(z, 0, 0).start()
     for way in (1, -1):
         ring_copy(0, way, 0).start()
     x_copy(z, 1, 1).start()
     for way in (1, -1):
         ring_copy(2, way, 0).start()
-    lax.fori_loop(1, Z, start_acts, 0)
-    own_cot.start()
-    pair_cot.start()
-
-    own_g.wait()
+    lax.fori_loop(1, Z, start_pair, 0)
     pair_g.wait_recv()
-    for r in range(Y):
-        take = pl.ds(pl.multiple_of(ring(y + r, Y) * QUARTER, QUARTER), QUARTER)
-        for b in range(2):
-            g_t[r * QUARTER : (r + 1) * QUARTER, b * TOK : (b + 1) * TOK] = (
-                g_buf[b, :, take].astype(F32).T.astype(BF16)
-            )
+    turned_g(1)
 
     A, B = slice(0, QUARTER // 2), slice(QUARTER // 2, QUARTER)
     half_rows = QUARTER // 2
@@ -291,57 +308,103 @@
                 here += plain(zr[j], zsr[j])
             fin[core * 4 + y], fin_scale[core * 4 + y] = coded(here)
 
-    def weights(t):
-        k = t // 2 + 1
-
-        @pl.when(t == 0)
-        def _():
-            arrive(z, 1 - x, 0)
+    def weights(i):
+        for flow, k, now in ((0, i // 2 + 1, i % 2 == 0), (1, i // 2, (i % 2 == 0) & (i > 0)), (2, (i + 1) // 2, i % 2 == 1)):
             for way in (1, -1):
-                ring_copy(1, way, 0).start()
-            pair_copy(z, 1 - x, 0).start()
-
-        for flow, parity in ((0, 0), (2, 0), (1, 1)):
-            for way in (1, -1):
-
-                @pl.when((t % 2 == parity) & (k <= HOPS[way][flow]))
+
+                @pl.when(now & (k <= HOPS[way][flow]))
                 def _():
                     ring_event(flow, way, k)
 
-        @pl.when(t == 1)
+    def weights_across(i):
+        @pl.when(i == 1)
         def _():
             x_event(1, 0)
 
         for way in (1, -1):
 
-            @pl.when((t % 2 == 1) & (k >= 2))
+            @pl.when((i % 2 == 1) & (i >= 3) & (i <= 7))
             def _():
-                x_event(way, k - 1)
-
-    def step(t, carry):
-        @pl.when(t < Z)
-        def _():
-            multiply(t)
-
-        @pl.when((t >= 1) & (t <= Z))
-        def _():
-            weights(t - 1)
-
-        @pl.when((t >= 2) & (t < Z + 2))
-        def _():
-            combine(t - 2)
-
-        @pl.when((t >= 3) & (t < Z + 3))
-        def _():
-            cross(t - 3)
-
-        @pl.when(t >= 4)
-        def _():
-            travel(t - 4)
-
-        return carry
-
-    lax.fori_loop(0, STEPS, step, 0)
+                x_event(way, (i - 1) // 2)
+
+    def adam(t):
+        at = pl.ds(pl.multiple_of(t * QUARTER, QUARTER), QUARTER)
+        gradient, master, moment, second = (key_buf[i, at] for i in range(4))
+        count = jnp.full((1, HALF), steps[0], I32).astype(F32)
+        moment_new = 0.9 * moment + 0.1 * gradient
+        second_new = 0.95 * second + 0.05 * gradient * gradient
+        first_fix = 1.0 - jnp.exp(count * LOG_KEEP_FIRST)
+        second_fix = 1.0 - jnp.exp(count * LOG_KEEP_SECOND)
+        key_out[0, at] = moment_new
+        key_out[1, at] = second_new
+        key_out[2, at] = moment_new / first_fix / (jnp.sqrt(second_new / second_fix) + 1e-08) + 0.1 * master
+
+    def product(i):
+        zo = ring(z + jnp.where(i % 2 == 1, (i + 1) // 2, -(i // 2)), Z)
+        for xo in range(2):
+
+            @pl.when(zo * 2 + xo != shard)
+            def _():
+                for half in range(2):
+                    at = block(zo, xo, half, 1 - core)
+                    remote(at, at, w_pair_send.at[0], w_pair_recv.at[mark(zo, xo, half)], to_pair).wait_recv()
+
+            to = pl.ds(pl.multiple_of((zo * 2 + xo) * 2 * HALF, 2 * HALF), 2 * HALF)
+            input_grad[:, to] = lax.dot_general(
+                cot[...], w[zo * 2 + xo], (((1,), (1,)), ((), ())), preferred_element_type=F32
+            ).astype(BF16)
+
+    def first(t, carry):
+        multiply(t)
+        return carry
+
+    def step(i, carry):
+        @pl.when(i < Z)
+        def _():
+            combine(i)
+
+        @pl.when(i + AHEAD < Z)
+        def _():
+            multiply(i + AHEAD)
+
+        @pl.when(i <= Z)
+        def _():
+            weights(i)
+
+        @pl.when((i >= CROSS_LAG) & (i < CROSS_LAG + Z))
+        def _():
+            cross(i - CROSS_LAG)
+
+        @pl.when(i >= TRAVEL_LAG)
+        def _():
+            travel(i - TRAVEL_LAG)
+
+        @pl.when(i < Z)
+        def _():
+            weights_across(i)
+            adam(i)
+
+        @pl.when((i >= 4) & (i < 7))
+        def _():
+            product(i - 4)
+
+        @pl.when((i >= 8) & (i < 10))
+        def _():
+            product(i - 5)
+
+        return carry
+
+    lax.fori_loop(0, AHEAD, first, 0)
+    arrive(z, 1 - x, 0)
+    for way in (1, -1):
+        ring_copy(1, way, 0).start()
+    pair_copy(z, 1 - x, 0).start()
+    for i in range(4):
+        key_copy(i).wait()
+    own_cot.wait()
+    other = cot.at[:, pl.ds(pl.multiple_of((1 - tensor) * 256, 256), 256)]
+    remote(pc, other, one.at[5], one.at[6], to_tensor).wait_recv()
+    lax.fori_loop(0, TRAVEL_LAG + Z, step, 0)
     x_event(1, 4)
 
     def fin_copy(r, of, device, send, recv):
@@ -360,16 +423,18 @@
     for r in (2, 1, 3):
         start(to_replica(r))
     start(to_partner(0))
+    def products(i, carry):
+        product(i)
+        return carry
+
+    lax.fori_loop(5, Z, products, 0)
     for r in (1, 3, 2):
         wait_recv(fin_copy(r, core, to_y(r), f_send, f_recv))
         start(to_partner(r))
     for r in range(Y):
         wait_recv(fin_copy(r, 1 - core, to_pair, fp_send, fp_recv))
 
-    own_cot.wait()
     pair_cot.wait_send()
-    other = cot.at[:, pl.ds(pl.multiple_of((1 - tensor) * 256, 256), 256)]
-    remote(pc, other, one.at[5], one.at[6], to_tensor).wait_recv()
     pair_g.wait_send()
 
     def finish(t, carry):
@@ -405,29 +470,38 @@
             x_copy(origin(way, k), 1, x_index(way, k)).wait_send()
 
     def finish_w(i, carry):
-        zo, xo, half = i // 4, (i // 2) % 2, i % 2
-
-        @pl.when(i // 2 != shard)
-        def _():
-            pair_copy(zo, xo, half).wait_send()
-            at = w.at[slot(zo, xo, half, 1 - core)]
-            remote(at, at, w_pair_send.at[i], w_pair_recv.at[i], to_pair).wait_recv()
-
-        return carry
-
-    lax.fori_loop(0, 4 * Z, finish_w, 0)
-
-
-def gathered(acts, g, pv, pc):
+        @pl.when(i != shard)
+        def _():
+            for half in range(2):
+                pair_copy(i // 2, i % 2, half).wait_send()
+
+        return carry
+
+    lax.fori_loop(0, 2 * Z, finish_w, 0)
+
+
+def gathered(steps, acts, g, pv, pc, keys):
     dma = pltpu.SemaphoreType.DMA
-    any_, vmem = pl.BlockSpec(memory_space=pl.ANY), pl.BlockSpec(memory_space=pltpu.VMEM)
-    S = jax.ShapeDtypeStruct
+    hbm, vmem = pl.BlockSpec(memory_space=pltpu.HBM), pl.BlockSpec(memory_space=pltpu.VMEM)
+    in_hbm = [pltpu.with_memory_space_constraint(v, pltpu.HBM) for v in (acts, g, pv, pc, *keys)]
+
+    def body(steps, acts, g, pv, pc, k0, k1, k2, k3, *rest):
+        exchange(steps, acts, g, pv, pc, (k0, k1, k2, k3), *rest)
+
     return pl.pallas_call(
-        exchange,
-        out_shape=(S((64, 128, 512), BF16), S((256, 512), BF16), S((8, QUARTER, HALF), I16), S((8, 1, HALF), F32)),
-        in_specs=[any_] * 4,
+        body,
+        out_shape=(
+            pltpu.VMEM((TOK, FEAT), BF16),
+            pltpu.VMEM((3, 1024, 256), F32),
+            pltpu.VMEM((8, QUARTER, HALF), I16),
+            pltpu.VMEM((8, 1, HALF), F32),
+        ),
+        in_specs=[pl.BlockSpec(memory_space=pltpu.SMEM)] + [hbm] * 8,
         out_specs=(vmem,) * 4,
         scratch_shapes=[
+            pltpu.VMEM((2 * Z, 2 * HALF, COLS), BF16),
+            pltpu.VMEM((TOK, COLS), BF16),
+            pltpu.VMEM((4, 1024, 256), F32),
             pltpu.VMEM((Z, TOK, 2 * HALF), BF16),
             pltpu.VMEM((Z, TOK, 2 * HALF), BF16),
             pltpu.VMEM((2, TOK, COLS), BF16),
@@ -441,16 +515,50 @@
             *[pltpu.VMEM((Z, 1, HALF), F32)] * 2,
             *[pltpu.VMEM((Z, QUARTER, HALF), I16)] * 2,
             *[pltpu.VMEM((Z, 1, HALF), F32)] * 2,
-            dma((Z, 2)), dma((Z, 2)), dma((Z, 2)), dma((7,)),
+            dma((4,)), dma((Z, 2)), dma((Z, 2)), dma((Z, 2)), dma((7,)),
             dma((32,)), dma((32,)), dma((2, 12)), dma((10,)), dma((32,)),
             dma((Z, 2, 2)), dma((Z, 2, 2)), dma((Z, 2, 2)), dma((Z, 2, 2)),
             dma((Z, 2)), dma((Z, 2)), dma((Z, 2)), dma((Z, 2)),
             dma((Y, 2)), dma((Y, 2)), dma((Y, 2)), dma((Y, 2)),
         ],
         compiler_params=pltpu.CompilerParams(
-            collective_id=1, has_side_effects=True, vmem_limit_bytes=48 << 20
+            collective_id=1, has_side_effects=True, vmem_limit_bytes=44 << 20
         ),
-    )(acts, g, pv.reshape(4, 128, 512), pc)
+    )(steps, *in_hbm)
+
+
+def write_out(input_grad, key_out, fin, fin_scale, value_to, moment_to, second_to, update_to, input_to, value_grad, sems):
+    copies = [
+        pltpu.make_async_copy(input_grad.at[pl.ds(i * 64, 64)], input_to.at[pl.ds(i * 64, 64)], sems.at[i])
+        for i in range(4)
+    ]
+    for i, to in enumerate((moment_to, second_to, update_to)):
+        copies.append(pltpu.make_async_copy(key_out.at[i], to, sems.at[4 + i]))
+    for copy in copies:
+        copy.start()
+    for core in range(2):
+        for y in range(Y):
+            value_grad[core * HALF : (core + 1) * HALF, y * QUARTER : (y + 1) * QUARTER] = plain(
+                fin[core * 4 + y], fin_scale[core * 4 + y]
+            ).T
+    last = pltpu.make_async_copy(value_grad, value_to, sems.at[7])
+    last.start()
+    for copy in copies:
+        copy.wait()
+    last.wait()
+
+
+def written(arrays):
+    S = jax.ShapeDtypeStruct
+    key = S((1024, 256), F32)
+    return pl.pallas_call(
+        write_out,
+        out_shape=(S((2 * HALF, COLS), F32), key, key, key, S((TOK, FEAT), BF16)),
+        in_specs=[pl.BlockSpec(memory_space=pltpu.VMEM)] * 4,
+        out_specs=(pl.BlockSpec(memory_space=pltpu.HBM),) * 5,
+        scratch_shapes=[pltpu.VMEM((2 * HALF, COLS), F32), pltpu.SemaphoreType.DMA((8,))],
+        compiler_params=pltpu.CompilerParams(vmem_limit_bytes=8 << 20),
+    )(*[pltpu.with_memory_space_constraint(v, pltpu.VMEM) for v in arrays])
 
 
 def local(
@@ -464,24 +572,10 @@
     previous_value,
     previous_cotangent,
 ):
-    weights, cotangent, fin, fin_scale = gathered(activations, value_cotangent, previous_value, previous_cotangent)
-    blocks = (fin.astype(F32) * fin_scale).reshape(2, Y, QUARTER, HALF)
-    value_grad = blocks.transpose(0, 3, 1, 2).reshape(2 * HALF, COLS)
-    moment_new = 0.9 * key_moment + 0.1 * key_gradient
-    second_new = 0.95 * key_second + 0.05 * key_gradient * key_gradient
-    steps_done = step_count.astype(jnp.float32)[0]
-    first_fix = 1.0 - jnp.power(jnp.float32(0.9), steps_done)
-    second_fix = 1.0 - jnp.power(jnp.float32(0.95), steps_done)
-    key_update = (
-        moment_new / first_fix / (jnp.sqrt(second_new / second_fix) + 1e-08) + 0.1 * key_master
-    )
-    input_grad = lax.dot_general(
-        cotangent,
-        weights.reshape(FEAT, COLS),
-        (((1,), (1,)), ((), ())),
-        preferred_element_type=jnp.float32,
-    ).astype(jnp.bfloat16)
-    return (value_grad, moment_new, second_new, key_update, input_grad)
+    keys = (key_gradient, key_master, key_moment, key_second)
+    return tuple(written(gathered(
+        step_count, activations, value_cotangent, previous_value, previous_cotangent, keys
+    )))
 
 
 def solution(mesh):

time: 92.2 us -> 72.5 us (0.79)
  matrix products: 7.86 us -> 0 us
  local copies, waits for them, and re-layouts: 6.5 us -> 0 us
  other arithmetic: 4.1 us -> 0 us
  Pallas kernels: 72.1 us -> 71.1 us
    dot_general x1 -> x0, matrix products: 7.86 us -> none  [local(): lax.dot_general(cotangent, weights.reshape(FEAT, COLS), (((1,), (1,)), ((...]
    unnamed x12 -> x0, local copies, waits for them, and re-layouts: 6.12 us -> none
    add x1 -> x0, other arithmetic: 3.92 us -> none  [local(): moment_new / first_fix / (jnp.sqrt(second_new / second_fix) + 1e-08)]
    pallas_call x1 -> x2, Pallas kernels: 72.1 us -> 71.1 us  [the longest x1 67.8 us: gathered(): pl.pallas_call(body, out_shape=(pltpu.VMEM((TOK, FEAT), BF16), pltpu.VMEM...]
where the time goes in v2:
time: 72.5 us; the launch traced here: 72.4 us
  Pallas kernels  71.1 us (98%)
  between operations  1.29 us (2%)
    pallas_call x1, Pallas kernels, gathered(): pl.pallas_call(body, out_shape=(pltpu.VMEM((TOK, FEAT), BF16), pltpu.VMEM...  67.8 us
    pallas_call x1, Pallas kernels, written(): pl.pallas_call(write_out, out_shape=(S((2 * HALF, COLS), F32), key, key,...  3.37 us

profile of v2, /device:TPU:1, one launch (start us, length us, event | category | flops | bytes accessed | tf_op | source)
XLA Modules:
  0.0 72.4 jit_solution(2491876824266519559)
XLA Ops:
  1.3 67.8 %shard_map.128 = (bf16[256,8192]{1,0:T(8,128)(2,1)S(1)}, f32[3,1024,256]{2,1,0:T(8,128)S(1)}, s16[8,128,256]{2,1,0:T(8,128)(2,1)S(1)}, f32[8,1,256]{2,1,0:T(1,128)S(1)}) custom-call(s32[1]{0:T(128)S(6)} %copy.14.steps, bf16[256,8192]{1,0:T(8,128)(2,1)} %acts.1, bf16[256,512]{1,0:T(8,128)(2,1)} %g.1, bf16[512,512]{1,0:T(8,128)(2,1)} %pv.1, ...), custom_call_target="tpu_custom_call" | custom-call | tf_op jit(solution)/shard_map/pallas_call | solution.py:491
  69.1 3.4 %shard_map.129 = (f32[512,512]{1,0:T(8,128)}, f32[1024,256]{1,0:T(8,128)}, f32[1024,256]{1,0:T(8,128)}, f32[1024,256]{1,0:T(8,128)}, bf16[256,8192]{1,0:T(8,128)(2,1)}) custom-call(bf16[256,8192]{1,0:T(8,128)(2,1)S(1)} %get-tuple-element.9.input_grad, f32[3,1024,256]{2,1,0:T(8,128)S(1)} %get-tuple-element.10.key_out, ...), custom_call_target="tpu_custom_call" | custom-call | tf_op jit(solution)/shard_map/pallas_call | solution.py:554

commit v3 on v2

v3 whole, which is shorter than its diff:
```python
import functools
import math

import jax
import jax.numpy as jnp
from jax import lax
from jax.experimental import pallas as pl
from jax.experimental.pallas import tpu as pltpu
from jax.sharding import PartitionSpec as P

MESH = pl.DeviceIdType.MESH
F32, BF16, I16, I32 = jnp.float32, jnp.bfloat16, jnp.int16, jnp.int32
Z, Y = 8, 4
TOK, FEAT, COLS = 256, 8192, 512
HALF = 256
QUARTER = COLS // Y
AHEAD = 3
CROSS_LAG, TRAVEL_LAG, WEIGHT_LAG = 2, 4, 1
SPLIT = 160
PARTS = ((0, SPLIT), (SPLIT, HALF - SPLIT))
ACROSS = 12
LOG_KEEP_FIRST, LOG_KEEP_SECOND = math.log(0.9), math.log(0.95)
HOPS = {1: (4, 3, 4), -1: (3, 4, 3)}


def coded(x):
    top = jnp.maximum(jnp.max(jnp.abs(x), axis=0, keepdims=True), 1e-30)
    return jnp.round(x * (32767.0 / top)).astype(I32).astype(I16), top * (1.0 / 32767.0)


def plain(q, scale):
    return q.astype(I32).astype(F32) * scale


def exchange(
    steps, acts, g, pv, pc, key_in,
    input_grad, key_out, fin, fin_scale,
    w, cot, key_buf, a_own, a_par, g_buf, g_t, part,
    m1s, m1r, m1ss, m1sr, m2s, m2r, m2ss, m2sr,
    xs, xr, xss, xsr, zs, zr, zss, zsr, tally,
    one, a_recv, w_recv, w_pair_recv, sent, m1_recv, m2_recv, x_recv, z_recv, f_recv,
):
    tensor = lax.axis_index("tensor")
    shard = lax.axis_index("shard")
    replica = lax.axis_index("replica")
    z, x = shard // 2, shard % 2
    y, core = replica // 2, replica % 2
    sgn = 1 - 2 * core

    def ring(at, n):
        return lax.rem(at + 2 * n, n)

    to_pair = (tensor, shard, y * 2 + 1 - core)
    to_x = (tensor, z * 2 + 1 - x, replica)
    to_tensor = (1 - tensor, shard, replica)

    def to_y(r):
        return (tensor, shard, ring(y + r, Y) * 2 + core)

    def to_z(way):
        return (tensor, ring(z + way * sgn, Z) * 2 + x, replica)

    def remote(src, dst, send, recv, device):
        return pltpu.make_async_remote_copy(
            src_ref=src, dst_ref=dst, send_sem=send, recv_sem=recv, device_id=device, device_id_type=MESH
        )

    def await_bytes(sem, *refs):
        for ref in refs:
            pltpu.make_async_copy(ref, ref, sem).wait()

    def units(n):
        return tally.at[pl.ds(0, n)]

    barrier = pltpu.get_barrier_semaphore()
    peers = (to_pair, to_x, to_tensor, to_y(1), to_y(2), to_y(3), to_z(1), to_z(-1))
    for peer in peers:
        pl.semaphore_signal(barrier, inc=1, device_id=peer, device_id_type=MESH)

    def columns(t, b, of_core):
        far = Z // 2 - (t + 1) // 2
        offset = jnp.where(t % 2 == 1, far, -far) * (1 - 2 * of_core)
        start = (ring(z + offset, Z) * 2 + b) * 2 * HALF + of_core * HALF
        return pl.ds(pl.multiple_of(start, HALF), HALF)

    def start_own(t, carry):
        for b in range(2):
            to = a_own.at[t, :, pl.ds(b * HALF, HALF)]
            pltpu.make_async_copy(acts.at[:, columns(t, b, core)], to, one.at[0]).start()
        return carry

    def start_pair(t, carry):
        for b in range(2):
            to = a_par.at[t, :, pl.ds(b * HALF, HALF)]
            remote(acts.at[:, columns(t, b, 1 - core)], to, sent.at[0], a_recv.at[t], to_pair).start()
        return carry

    own_g = pltpu.make_async_copy(g, g_buf.at[0], one.at[1])
    pair_g = remote(g, g_buf.at[1], one.at[2], one.at[3], to_pair)
    own_w = pltpu.make_async_copy(pv, w.at[pl.ds(pl.multiple_of(shard * 2 * HALF, 2 * HALF), 2 * HALF)], one.at[4])
    cot_at = cot.at[:, pl.ds(pl.multiple_of(tensor * 256, 256), 256)]
    own_cot = pltpu.make_async_copy(pc, cot_at, one.at[5])
    pair_cot = remote(pc, cot_at, one.at[6], one.at[7], to_tensor)

    def block(zo, xo, half):
        first, count = PARTS[half]
        return w.at[pl.ds(pl.multiple_of((zo * 2 + xo) * 2 * HALF + core * HALF + first, 16), count)]

    def own_block(half):
        first, count = PARTS[half]
        return pv.at[pl.ds(pl.multiple_of(core * HALF + first, 16), count)]

    def flow_of(flow):
        return (1 - x if flow == 1 else x), (1 if flow == 2 else 0)

    def origin(way, k):
        return ring(z - way * sgn * k, Z)

    def ring_send(flow, way, k, source=None):
        xo, half = flow_of(flow)
        at = block(origin(way, k), xo, half)
        remote(at if source is None else source, at, sent.at[1], w_recv.at[flow * 4 + k], to_z(way)).start()

    def x_send(zo, half, mark, source=None):
        at = block(zo, x, half)
        remote(at if source is None else source, at, sent.at[2], w_recv.at[mark], to_x).start()

    def pair_send(zo, xo, half):
        at = block(zo, xo, half)
        remote(at, at, sent.at[3], w_pair_recv.at[zo], to_pair).start()

    def arrive(mark, half, count):
        await_bytes(w_recv.at[mark], w.at[pl.ds(0, count * PARTS[half][1])])

    def ring_events(flow, k, ways):
        xo, half = flow_of(flow)
        arrive(flow * 4 + k - 1, half, len(ways))
        for way in ways:

            @pl.when(k < HOPS[way][flow])
            def _():
                ring_send(flow, way, k)

        for way in ways:
            zo = origin(way, k)
            if flow == 2:
                x_send(zo, half, ACROSS + 1 + k)
            pair_send(zo, xo, half)

    def x_events(k, ways):
        arrive(ACROSS + 1 + k, 1, len(ways))
        for way in ways:
            pair_send(origin(way, k), 1 - x, 1)

    def turned_g(b):
        for r in range(Y):
            take = pl.ds(pl.multiple_of(ring(y + r, Y) * QUARTER, QUARTER), QUARTER)
            g_t[r * QUARTER : (r + 1) * QUARTER, b * TOK : (b + 1) * TOK] = (
                g_buf[b, :, take].astype(F32).T.astype(BF16)
            )

    own_g.start()
    lax.fori_loop(0, Z, start_own, 0)
    pl.semaphore_wait(barrier, len(peers))
    pair_g.start()
    lax.fori_loop(0, 1, start_pair, 0)
    x_send(z, 0, ACROSS, own_block(0))
    for way in (1, -1):
        ring_send(0, way, 0, own_block(0))
    pair_cot.start()
    x_send(z, 1, ACROSS + 1, own_block(1))
    for way in (1, -1):
        ring_send(2, way, 0, own_block(1))
    lax.fori_loop(1, Z, start_pair, 0)
    own_w.start()
    own_cot.start()
    for i in range(4):
        pltpu.make_async_copy(key_in[i], key_buf.at[i], one.at[8]).start()
    own_g.wait()
    turned_g(0)
    await_bytes(one.at[0], a_own)

    A, B = slice(0, QUARTER // 2), slice(QUARTER // 2, QUARTER)
    half_rows = QUARTER // 2

    def rows(r, first=0, count=QUARTER):
        return pl.ds(r * QUARTER + first, count)

    def send_y(src, dst, src_scale, dst_scale, send, recv, t):
        for way in range(2):
            to = to_y(1 if way == 0 else 3)
            remote(src.at[t, way], dst.at[t, way], sent.at[send], recv.at[t], to).start()
            remote(src_scale.at[t, way], dst_scale.at[t, way], sent.at[send + 1], recv.at[t], to).start()

    def send_z(j, way, first=0, count=QUARTER):
        some = pl.ds(first, count)
        remote(zs.at[j, some], zr.at[j, some], sent.at[10], z_recv.at[j], to_z(way)).start()
        remote(zss.at[j], zsr.at[j], sent.at[11], z_recv.at[j], to_z(way)).start()

    def multiply_own(t):
        part[t] = jnp.dot(g_t[:, :TOK], a_own[t], preferred_element_type=F32)

    def multiply(t):
        await_bytes(a_recv.at[t], a_par.at[t])
        part[t] += jnp.dot(g_t[:, TOK:], a_par[t], preferred_element_type=F32)
        up = jnp.concatenate([part[t, rows(2, 0, half_rows)], part[t, rows(1, half_rows, half_rows)]], axis=0)
        m1s[t, 0], m1ss[t, 0] = coded(up)
        down = jnp.concatenate([part[t, rows(2, half_rows, half_rows)], part[t, rows(3, 0, half_rows)]], axis=0)
        m1s[t, 1], m1ss[t, 1] = coded(down)
        send_y(m1s, m1r, m1ss, m1sr, 4, m1_recv, t)

    def combine(t):
        await_bytes(m1_recv.at[t], units(260))
        above, below = plain(m1r[t, 0], m1sr[t, 0]), plain(m1r[t, 1], m1sr[t, 1])
        m2s[t, 0], m2ss[t, 0] = coded(part[t, rows(1, 0, half_rows)] + above[A])
        m2s[t, 1], m2ss[t, 1] = coded(part[t, rows(3, half_rows, half_rows)] + below[A])
        send_y(m2s, m2r, m2ss, m2sr, 6, m2_recv, t)
        part[t, rows(0, half_rows, half_rows)] += above[B]
        part[t, rows(0, 0, half_rows)] += below[B]

    def cross(t):
        await_bytes(m2_recv.at[t], units(132))
        part[t, rows(0, 0, half_rows)] += plain(m2r[t, 0], m2sr[t, 0])
        part[t, rows(0, half_rows, half_rows)] += plain(m2r[t, 1], m2sr[t, 1])
        xs[t], xss[t] = coded(part[t, rows(0), pl.ds(pl.multiple_of((1 - x) * HALF, HALF), HALF)])
        remote(xs.at[t], xr.at[t], sent.at[8], x_recv.at[t], to_x).start()
        remote(xss.at[t], xsr.at[t], sent.at[9], x_recv.at[t], to_x).start()

    def crossed(t):
        await_bytes(x_recv.at[t], units(65))
        return part[t, rows(0), pl.ds(pl.multiple_of(x * HALF, HALF), HALF)] + plain(xr[t], xsr[t])

    def travel(t):
        @pl.when(t == 0)
        def _():
            here = crossed(0)
            zs[0, A], zss[0] = coded(here[A])
            send_z(0, 1, 0, half_rows)
            zs[1, B], zss[1] = coded(here[B])
            send_z(1, -1, half_rows, half_rows)

        @pl.when(t == 1)
        def _():
            here = crossed(1)
            await_bytes(z_recv.at[0], units(33))
            zs[2], zss[2] = coded(jnp.concatenate([here[A] + plain(zr[0, A], zsr[0]), here[B]], axis=0))
            send_z(2, 1)

        @pl.when(t == 2)
        def _():
            here = crossed(2)
            await_bytes(z_recv.at[1], units(33))
            zs[3], zss[3] = coded(jnp.concatenate([here[A], here[B] + plain(zr[1, B], zsr[1])], axis=0))
            send_z(3, -1)

        for way in (1, -1):

            @pl.when((t >= 3) & (t <= 6) & (t % 2 == (1 if way == 1 else 0)))
            def _():
                here = crossed(t)
                await_bytes(z_recv.at[t - 1], units(65))
                zs[t + 1], zss[t + 1] = coded(here + plain(zr[t - 1], zsr[t - 1]))
                send_z(t + 1, way)

        @pl.when(t == 7)
        def _():
            here = crossed(7)
            for j in (6, 7):
                await_bytes(z_recv.at[j], units(65))
                here += plain(zr[j], zsr[j])
            fin[core * 4 + y], fin_scale[core * 4 + y] = coded(here)

    def weights(i):
        both = (1, -1)
        for flow, k, now in ((0, i // 2 + 1, i % 2 == 0), (1, i // 2, (i % 2 == 0) & (i > 0)), (2, (i + 1) // 2, i % 2 == 1)):

            @pl.when(now & (k < 4))
            def _():
                ring_events(flow, k, both)

            @pl.when(now & (k == 4))
            def _():
                ring_events(flow, 4, tuple(way for way in both if HOPS[way][flow] == 4))

    def weights_across(i):
        @pl.when(i == 1)
        def _():
            x_events(0, (1,))

        @pl.when((i % 2 == 1) & (i >= 3) & (i <= 7))
        def _():
            x_events((i - 1) // 2, (1, -1))

    def adam(t):
        at = pl.ds(pl.multiple_of(t * QUARTER, QUARTER), QUARTER)
        gradient, master, moment, second = (key_buf[i, at] for i in range(4))
        count = jnp.full((1, HALF), steps[0], I32).astype(F32)
        moment_new = 0.9 * moment + 0.1 * gradient
        second_new = 0.95 * second + 0.05 * gradient * gradient
        first_fix = 1.0 - jnp.exp(count * LOG_KEEP_FIRST)
        second_fix = 1.0 - jnp.exp(count * LOG_KEEP_SECOND)
        key_out[0, at] = moment_new
        key_out[1, at] = second_new
        key_out[2, at] = moment_new / first_fix / (jnp.sqrt(second_new / second_fix) + 1e-08) + 0.1 * master

    def product(i):
        zo = ring(z + jnp.where(i % 2 == 1, (i + 1) // 2, -(i // 2)), Z)

        @pl.when(i == 0)
        def _():
            await_bytes(w_pair_recv.at[zo], w.at[pl.ds(0, HALF)])

        @pl.when(i > 0)
        def _():
            await_bytes(w_pair_recv.at[zo], w.at[pl.ds(0, 2 * HALF)])

        for xo in range(2):
            at = pl.ds(pl.multiple_of((zo * 2 + xo) * 2 * HALF, 2 * HALF), 2 * HALF)
            input_grad[:, at] = lax.dot_general(
                cot[...], w[at], (((1,), (1,)), ((), ())), preferred_element_type=F32
            ).astype(BF16)

    def loop(first, last, body):
        def step(i, carry):
            body(i)
            return carry

        lax.fori_loop(first, last, step, 0)

    def step(i):
        @pl.when(i < Z)
        def _():
            combine(i)

        @pl.when(i + AHEAD < Z)
        def _():
            multiply_own(i + AHEAD)
            multiply(i + AHEAD)

        @pl.when((i >= CROSS_LAG) & (i < CROSS_LAG + Z))
        def _():
            cross(i - CROSS_LAG)

        @pl.when(i >= TRAVEL_LAG)
        def _():
            travel(i - TRAVEL_LAG)

        @pl.when((i >= WEIGHT_LAG) & (i <= WEIGHT_LAG + Z))
        def _():
            weights(i - WEIGHT_LAG)
            weights_across(i - WEIGHT_LAG)

        @pl.when(i < Z)
        def _():
            adam(i)

        @pl.when(i == 4)
        def _():
            product(0)

        @pl.when((i == 6) | (i == 7))
        def _():
            product(i - 5)

    loop(0, AHEAD, multiply_own)
    pair_g.wait_recv()
    turned_g(1)
    loop(0, AHEAD, multiply)
    await_bytes(one.at[8], key_buf)
    own_w.wait()
    arrive(ACROSS, 0, 1)
    for way in (1, -1):
        ring_send(1, way, 0)
    pair_send(z, 1 - x, 0)
    own_cot.wait()
    pair_cot.wait_recv()
    loop(0, TRAVEL_LAG + Z, step)

    def send_fin(at, send, recv, device):
        remote(fin.at[at], fin.at[at], sent.at[send], recv, device).start()
        remote(fin_scale.at[at], fin_scale.at[at], sent.at[send + 1], recv, device).start()

    for r in (2, 1, 3):
        send_fin(core * 4 + y, 12, f_recv.at[r], to_y(r))
    send_fin(core * 4 + y, 14, f_recv.at[0], to_pair)
    x_events(4, (1,))
    loop(3, Z, product)
    for r in (1, 3, 2):
        await_bytes(f_recv.at[r], units(65))
        send_fin(core * 4 + ring(y - r, Y), 14, f_recv.at[0], to_pair)

    pair_cot.wait_send()
    pair_g.wait_send()
    await_bytes(sent.at[0], a_par)
    await_bytes(sent.at[1], w.at[pl.ds(0, 14 * SPLIT + 7 * (HALF - SPLIT))])
    await_bytes(sent.at[2], w.at[pl.ds(0, SPLIT + Z * (HALF - SPLIT))])
    await_bytes(sent.at[3], w.at[pl.ds(0, (2 * Z - 1) * HALF)])
    for i, ref in enumerate((m1s, m1ss, m2s, m2ss, xs, xss, zs.at[pl.ds(0, Z - 1)], zss)):
        await_bytes(sent.at[4 + i], ref)
    for i, ref in enumerate((fin.at[pl.ds(0, 3)], fin_scale.at[pl.ds(0, 3)], fin.at[pl.ds(0, 4)], fin_scale.at[pl.ds(0, 4)])):
        await_bytes(sent.at[12 + i], ref)
    await_bytes(f_recv.at[0], units(260))


def gathered(steps, acts, g, pv, pc, keys):
    dma = pltpu.SemaphoreType.DMA
    hbm, vmem = pl.BlockSpec(memory_space=pltpu.HBM), pl.BlockSpec(memory_space=pltpu.VMEM)
    in_hbm = [pltpu.with_memory_space_constraint(v, pltpu.HBM) for v in (acts, g, pv, pc, *keys)]

    def body(steps, acts, g, pv, pc, k0, k1, k2, k3, *rest):
        exchange(steps, acts, g, pv, pc, (k0, k1, k2, k3), *rest)

    return pl.pallas_call(
        body,
        out_shape=(
            pltpu.VMEM((TOK, FEAT), BF16),
            pltpu.VMEM((3, 1024, 256), F32),
            pltpu.VMEM((8, QUARTER, HALF), I16),
            pltpu.VMEM((8, 1, HALF), F32),
        ),
        in_specs=[pl.BlockSpec(memory_space=pltpu.SMEM)] + [hbm] * 8,
        out_specs=(vmem,) * 4,
        scratch_shapes=[
            pltpu.VMEM((FEAT, COLS), BF16),
            pltpu.VMEM((TOK, COLS), BF16),
            pltpu.VMEM((4, 1024, 256), F32),
            pltpu.VMEM((Z, TOK, 2 * HALF), BF16),
            pltpu.VMEM((Z, TOK, 2 * HALF), BF16),
            pltpu.VMEM((2, TOK, COLS), BF16),
            pltpu.VMEM((COLS, 2 * TOK), BF16),
            pltpu.VMEM((Z, COLS, 2 * HALF), F32),
            *[pltpu.VMEM((Z, 2, QUARTER, 2 * HALF), I16)] * 2,
            *[pltpu.VMEM((Z, 2, 1, 2 * HALF), F32)] * 2,
            *[pltpu.VMEM((Z, 2, QUARTER // 2, 2 * HALF), I16)] * 2,
            *[pltpu.VMEM((Z, 2, 1, 2 * HALF), F32)] * 2,
            *[pltpu.VMEM((Z, QUARTER, HALF), I16)] * 2,
            *[pltpu.VMEM((Z, 1, HALF), F32)] * 2,
            *[pltpu.VMEM((Z, QUARTER, HALF), I16)] * 2,
            *[pltpu.VMEM((Z, 1, HALF), F32)] * 2,
            pltpu.VMEM((260, 1, HALF), F32),
            dma((9,)), dma((Z,)), dma((18,)), dma((Z,)), dma((16,)),
            dma((Z,)), dma((Z,)), dma((Z,)), dma((Z,)), dma((Y,)),
        ],
        compiler_params=pltpu.CompilerParams(
            collective_id=1, has_side_effects=True, vmem_limit_bytes=44 << 20
        ),
    )(steps, *in_hbm)


def write_out(input_grad, key_out, fin, fin_scale, value_to, moment_to, second_to, update_to, input_to, value_grad, sems):
    copies = [
        pltpu.make_async_copy(input_grad.at[pl.ds(i * 64, 64)], input_to.at[pl.ds(i * 64, 64)], sems.at[i])
        for i in range(4)
    ]
    for i, to in enumerate((moment_to, second_to, update_to)):
        copies.append(pltpu.make_async_copy(key_out.at[i], to, sems.at[4 + i]))
    for copy in copies:
        copy.start()
    for core in range(2):
        for y in range(Y):
            value_grad[core * HALF : (core + 1) * HALF, y * QUARTER : (y + 1) * QUARTER] = plain(
                fin[core * 4 + y], fin_scale[core * 4 + y]
            ).T
    last = pltpu.make_async_copy(value_grad, value_to, sems.at[7])
    last.start()
    for copy in copies:
        copy.wait()
    last.wait()


def written(arrays):
    S = jax.ShapeDtypeStruct
    key = S((1024, 256), F32)
    return pl.pallas_call(
        write_out,
        out_shape=(S((2 * HALF, COLS), F32), key, key, key, S((TOK, FEAT), BF16)),
        in_specs=[pl.BlockSpec(memory_space=pltpu.VMEM)] * 4,
        out_specs=(pl.BlockSpec(memory_space=pltpu.HBM),) * 5,
        scratch_shapes=[pltpu.VMEM((2 * HALF, COLS), F32), pltpu.SemaphoreType.DMA((8,))],
        compiler_params=pltpu.CompilerParams(vmem_limit_bytes=8 << 20),
    )(*[pltpu.with_memory_space_constraint(v, pltpu.VMEM) for v in arrays])


def local(
    activations,
    value_cotangent,
    key_gradient,
    key_master,
    key_moment,
    key_second,
    step_count,
    previous_value,
    previous_cotangent,
):
    keys = (key_gradient, key_master, key_moment, key_second)
    return tuple(written(gathered(
        step_count, activations, value_cotangent, previous_value, previous_cotangent, keys
    )))


def solution(mesh):
    in_specs = (
        P(("shard", "replica"), "tensor"),
        P(("shard", "replica"), None),
        P("shard", "tensor"),
        P("shard", "tensor"),
        P("shard", "tensor"),
        P("shard", "tensor"),
        P(),
        P(("tensor", "shard"), None),
        P(("shard", "replica"), "tensor"),
    )
    out_specs = (
        P(("tensor", "shard"), None),
        P("shard", "tensor"),
        P("shard", "tensor"),
        P("shard", "tensor"),
        P(("shard", "replica"), "tensor"),
    )
    return jax.shard_map(local, mesh=mesh, in_specs=in_specs, out_specs=out_specs, check_vma=False)
```

time: 72.5 us -> 67.8 us (0.935)
  Pallas kernels: 71.1 us -> 66.4 us
    pallas_call x1, Pallas kernels: 67.8 us -> 63.1 us  [gathered(): pl.pallas_call(body, out_shape=(pltpu.VMEM((TOK, FEAT), BF16), pltpu.VMEM...]
where the time goes in v3:
time: 67.8 us; the launch traced here: 67.7 us
  Pallas kernels  66.4 us (98%)
  between operations  1.29 us (2%)
    pallas_call x1, Pallas kernels, gathered(): pl.pallas_call(body, out_shape=(pltpu.VMEM((TOK, FEAT), BF16), pltpu.VMEM...  63.1 us
    pallas_call x1, Pallas kernels, written(): pl.pallas_call(write_out, out_shape=(S((2 * HALF, COLS), F32), key, key,...  3.37 us

profile of v3, /device:TPU:1, one launch (start us, length us, event | category | flops | bytes accessed | tf_op | source)
XLA Modules:
  0.0 67.7 jit_solution(9838330288284969969)
XLA Ops:
  1.3 63.1 %shard_map.128 = (bf16[256,8192]{1,0:T(8,128)(2,1)S(1)}, f32[3,1024,256]{2,1,0:T(8,128)S(1)}, s16[8,128,256]{2,1,0:T(8,128)(2,1)S(1)}, f32[8,1,256]{2,1,0:T(1,128)S(1)}) custom-call(s32[1]{0:T(128)S(6)} %copy.14.steps, bf16[256,8192]{1,0:T(8,128)(2,1)} %acts.1, bf16[256,512]{1,0:T(8,128)(2,1)} %g.1, bf16[512,512]{1,0:T(8,128)(2,1)} %pv.1, ...), custom_call_target="tpu_custom_call" | custom-call | tf_op jit(solution)/shard_map/pallas_call | solution.py:413
  64.4 3.4 %shard_map.129 = (f32[512,512]{1,0:T(8,128)}, f32[1024,256]{1,0:T(8,128)}, f32[1024,256]{1,0:T(8,128)}, f32[1024,256]{1,0:T(8,128)}, bf16[256,8192]{1,0:T(8,128)(2,1)}) custom-call(bf16[256,8192]{1,0:T(8,128)(2,1)S(1)} %get-tuple-element.9.input_grad, f32[3,1024,256]{2,1,0:T(8,128)S(1)} %get-tuple-element.10.key_out, ...), custom_call_target="tpu_custom_call" | custom-call | tf_op jit(solution)/shard_map/pallas_call | solution.py:474

commit v4 on v3

--- a/solution.py
+++ b/solution.py
@@ -14,9 +14,8 @@
 TOK, FEAT, COLS = 256, 8192, 512
 HALF = 256
 QUARTER = COLS // Y
-AHEAD = 3
-CROSS_LAG, TRAVEL_LAG, WEIGHT_LAG = 2, 4, 1
-SPLIT = 160
+EARLY = 6
+SPLIT = 192
 PARTS = ((0, SPLIT), (SPLIT, HALF - SPLIT))
 ACROSS = 12
 LOG_KEEP_FIRST, LOG_KEEP_SECOND = math.log(0.9), math.log(0.95)
@@ -35,9 +34,10 @@
 def exchange(
     steps, acts, g, pv, pc, key_in,
     input_grad, key_out, fin, fin_scale,
-    w, cot, key_buf, a_own, a_par, g_buf, g_t, part,
+    w, cot, relay, key_buf, a_own, a_par, g_buf, g_t, part,
     m1s, m1r, m1ss, m1sr, m2s, m2r, m2ss, m2sr,
-    xs, xr, xss, xsr, zs, zr, zss, zsr, tally,
+    xs, xr, xss, xsr, zs, zr, zss, zsr,
+    n1s, n1r, n1ss, n1sr, n2s, n2r, n2ss, n2sr, es, er, ess, esr, tally,
     one, a_recv, w_recv, w_pair_recv, sent, m1_recv, m2_recv, x_recv, z_recv, f_recv,
 ):
     tensor = lax.axis_index("tensor")
@@ -52,7 +52,7 @@
 
     to_pair = (tensor, shard, y * 2 + 1 - core)
     to_x = (tensor, z * 2 + 1 - x, replica)
-    to_tensor = (1 - tensor, shard, replica)
+    to_next = (1 - tensor, z * 2 + 1 - x, replica)
 
     def to_y(r):
         return (tensor, shard, ring(y + r, Y) * 2 + core)
@@ -73,7 +73,7 @@
         return tally.at[pl.ds(0, n)]
 
     barrier = pltpu.get_barrier_semaphore()
-    peers = (to_pair, to_x, to_tensor, to_y(1), to_y(2), to_y(3), to_z(1), to_z(-1))
+    peers = (to_pair, to_x, to_next, to_y(1), to_y(2), to_y(3), to_z(1), to_z(-1))
     for peer in peers:
         pl.semaphore_signal(barrier, inc=1, device_id=peer, device_id_type=MESH)
 
@@ -100,7 +100,8 @@
     own_w = pltpu.make_async_copy(pv, w.at[pl.ds(pl.multiple_of(shard * 2 * HALF, 2 * HALF), 2 * HALF)], one.at[4])
     cot_at = cot.at[:, pl.ds(pl.multiple_of(tensor * 256, 256), 256)]
     own_cot = pltpu.make_async_copy(pc, cot_at, one.at[5])
-    pair_cot = remote(pc, cot_at, one.at[6], one.at[7], to_tensor)
+    next_cot = remote(pc, relay, one.at[6], one.at[7], to_next)
+    far_cot = remote(relay, cot.at[:, pl.ds(pl.multiple_of((1 - tensor) * 256, 256), 256)], one.at[9], one.at[10], to_x)
 
     def block(zo, xo, half):
         first, count = PARTS[half]
@@ -136,9 +137,7 @@
         xo, half = flow_of(flow)
         arrive(flow * 4 + k - 1, half, len(ways))
         for way in ways:
-
-            @pl.when(k < HOPS[way][flow])
-            def _():
+            if k < HOPS[way][flow]:
                 ring_send(flow, way, k)
 
         for way in ways:
@@ -167,7 +166,6 @@
     x_send(z, 0, ACROSS, own_block(0))
     for way in (1, -1):
         ring_send(0, way, 0, own_block(0))
-    pair_cot.start()
     x_send(z, 1, ACROSS + 1, own_block(1))
     for way in (1, -1):
         ring_send(2, way, 0, own_block(1))
@@ -189,8 +187,8 @@
     def send_y(src, dst, src_scale, dst_scale, send, recv, t):
         for way in range(2):
             to = to_y(1 if way == 0 else 3)
-            remote(src.at[t, way], dst.at[t, way], sent.at[send], recv.at[t], to).start()
-            remote(src_scale.at[t, way], dst_scale.at[t, way], sent.at[send + 1], recv.at[t], to).start()
+            remote(src.at[t, way], dst.at[t, way], sent.at[send], recv, to).start()
+            remote(src_scale.at[t, way], dst_scale.at[t, way], sent.at[send + 1], recv, to).start()
 
     def send_z(j, way, first=0, count=QUARTER):
         some = pl.ds(first, count)
@@ -200,96 +198,100 @@
     def multiply_own(t):
         part[t] = jnp.dot(g_t[:, :TOK], a_own[t], preferred_element_type=F32)
 
-    def multiply(t):
+    own_lanes = pl.ds(pl.multiple_of(x * HALF, HALF), HALF)
+    other_lanes = pl.ds(pl.multiple_of((1 - x) * HALF, HALF), HALF)
+    y_first = (m1s, m1r, m1ss, m1sr, 4), (m2s, m2r, m2ss, m2sr, 6)
+    x_first = (n1s, n1r, n1ss, n1sr, 16), (n2s, n2r, n2ss, n2sr, 18)
+
+    def route(t):
+        return (*y_first, t, slice(None)) if t < EARLY else (*x_first, t - EARLY, own_lanes)
+
+    def multiply_pair(t):
         await_bytes(a_recv.at[t], a_par.at[t])
         part[t] += jnp.dot(g_t[:, TOK:], a_par[t], preferred_element_type=F32)
-        up = jnp.concatenate([part[t, rows(2, 0, half_rows)], part[t, rows(1, half_rows, half_rows)]], axis=0)
-        m1s[t, 0], m1ss[t, 0] = coded(up)
-        down = jnp.concatenate([part[t, rows(2, half_rows, half_rows)], part[t, rows(3, 0, half_rows)]], axis=0)
-        m1s[t, 1], m1ss[t, 1] = coded(down)
-        send_y(m1s, m1r, m1ss, m1sr, 4, m1_recv, t)
+
+    def cross_early(t):
+        multiply_own(t)
+        multiply_pair(t)
+        e = t - EARLY
+        for r in range(Y):
+            es[e, rows(r)], ess[e, r] = coded(part[t, rows(r), other_lanes])
+        remote(es.at[e], er.at[e], sent.at[8], x_recv.at[t], to_x).start()
+        remote(ess.at[e], esr.at[e], sent.at[9], x_recv.at[t], to_x).start()
+
+    def send_first(t):
+        (src, dst, src_scale, dst_scale, send), _, at, lanes = route(t)
+        if t >= EARLY:
+            await_bytes(x_recv.at[t], units(260))
+            for r in range(Y):
+                part[t, rows(r), lanes] += plain(er[at, rows(r)], esr[at, r])
+        up = jnp.concatenate([part[t, rows(2, 0, half_rows), lanes], part[t, rows(1, half_rows, half_rows), lanes]], axis=0)
+        src[at, 0], src_scale[at, 0] = coded(up)
+        down = jnp.concatenate([part[t, rows(2, half_rows, half_rows), lanes], part[t, rows(3, 0, half_rows), lanes]], axis=0)
+        src[at, 1], src_scale[at, 1] = coded(down)
+        send_y(src, dst, src_scale, dst_scale, send, m1_recv.at[t], at)
+
+    def multiply(t):
+        multiply_pair(t)
+        send_first(t)
 
     def combine(t):
-        await_bytes(m1_recv.at[t], units(260))
-        above, below = plain(m1r[t, 0], m1sr[t, 0]), plain(m1r[t, 1], m1sr[t, 1])
-        m2s[t, 0], m2ss[t, 0] = coded(part[t, rows(1, 0, half_rows)] + above[A])
-        m2s[t, 1], m2ss[t, 1] = coded(part[t, rows(3, half_rows, half_rows)] + below[A])
-        send_y(m2s, m2r, m2ss, m2sr, 6, m2_recv, t)
-        part[t, rows(0, half_rows, half_rows)] += above[B]
-        part[t, rows(0, 0, half_rows)] += below[B]
+        (_, got, _, got_scale, _), (src, dst, src_scale, dst_scale, send), at, lanes = route(t)
+        await_bytes(m1_recv.at[t], units(260 if t < EARLY else 130))
+        above, below = plain(got[at, 0], got_scale[at, 0]), plain(got[at, 1], got_scale[at, 1])
+        src[at, 0], src_scale[at, 0] = coded(part[t, rows(1, 0, half_rows), lanes] + above[A])
+        src[at, 1], src_scale[at, 1] = coded(part[t, rows(3, half_rows, half_rows), lanes] + below[A])
+        send_y(src, dst, src_scale, dst_scale, send, m2_recv.at[t], at)
+        part[t, rows(0, half_rows, half_rows), lanes] += above[B]
+        part[t, rows(0, 0, half_rows), lanes] += below[B]
 
     def cross(t):
-        await_bytes(m2_recv.at[t], units(132))
-        part[t, rows(0, 0, half_rows)] += plain(m2r[t, 0], m2sr[t, 0])
-        part[t, rows(0, half_rows, half_rows)] += plain(m2r[t, 1], m2sr[t, 1])
-        xs[t], xss[t] = coded(part[t, rows(0), pl.ds(pl.multiple_of((1 - x) * HALF, HALF), HALF)])
-        remote(xs.at[t], xr.at[t], sent.at[8], x_recv.at[t], to_x).start()
-        remote(xss.at[t], xsr.at[t], sent.at[9], x_recv.at[t], to_x).start()
+        _, (_, got, _, got_scale, _), at, lanes = route(t)
+        await_bytes(m2_recv.at[t], units(132 if t < EARLY else 66))
+        part[t, rows(0, 0, half_rows), lanes] += plain(got[at, 0], got_scale[at, 0])
+        part[t, rows(0, half_rows, half_rows), lanes] += plain(got[at, 1], got_scale[at, 1])
+        if t < EARLY:
+            xs[t], xss[t] = coded(part[t, rows(0), other_lanes])
+            remote(xs.at[t], xr.at[t], sent.at[20], x_recv.at[t], to_x).start()
+            remote(xss.at[t], xsr.at[t], sent.at[21], x_recv.at[t], to_x).start()
 
     def crossed(t):
-        await_bytes(x_recv.at[t], units(65))
-        return part[t, rows(0), pl.ds(pl.multiple_of(x * HALF, HALF), HALF)] + plain(xr[t], xsr[t])
+        here = part[t, rows(0), own_lanes]
+        if t < EARLY:
+            await_bytes(x_recv.at[t], units(65))
+            here += plain(xr[t], xsr[t])
+        return here
 
     def travel(t):
-        @pl.when(t == 0)
-        def _():
-            here = crossed(0)
+        here = crossed(t)
+        if t == 0:
             zs[0, A], zss[0] = coded(here[A])
             send_z(0, 1, 0, half_rows)
             zs[1, B], zss[1] = coded(here[B])
             send_z(1, -1, half_rows, half_rows)
-
-        @pl.when(t == 1)
-        def _():
-            here = crossed(1)
+        elif t == 1:
             await_bytes(z_recv.at[0], units(33))
             zs[2], zss[2] = coded(jnp.concatenate([here[A] + plain(zr[0, A], zsr[0]), here[B]], axis=0))
             send_z(2, 1)
-
-        @pl.when(t == 2)
-        def _():
-            here = crossed(2)
+        elif t == 2:
             await_bytes(z_recv.at[1], units(33))
             zs[3], zss[3] = coded(jnp.concatenate([here[A], here[B] + plain(zr[1, B], zsr[1])], axis=0))
             send_z(3, -1)
-
-        for way in (1, -1):
-
-            @pl.when((t >= 3) & (t <= 6) & (t % 2 == (1 if way == 1 else 0)))
-            def _():
-                here = crossed(t)
-                await_bytes(z_recv.at[t - 1], units(65))
-                zs[t + 1], zss[t + 1] = coded(here + plain(zr[t - 1], zsr[t - 1]))
-                send_z(t + 1, way)
-
-        @pl.when(t == 7)
-        def _():
-            here = crossed(7)
+        elif t < 7:
+            await_bytes(z_recv.at[t - 1], units(65))
+            zs[t + 1], zss[t + 1] = coded(here + plain(zr[t - 1], zsr[t - 1]))
+            send_z(t + 1, 1 if t % 2 else -1)
+        else:
             for j in (6, 7):
                 await_bytes(z_recv.at[j], units(65))
                 here += plain(zr[j], zsr[j])
             fin[core * 4 + y], fin_scale[core * 4 + y] = coded(here)
 
-    def weights(i):
-        both = (1, -1)
-        for flow, k, now in ((0, i // 2 + 1, i % 2 == 0), (1, i // 2, (i % 2 == 0) & (i > 0)), (2, (i + 1) // 2, i % 2 == 1)):
-
-            @pl.when(now & (k < 4))
-            def _():
-                ring_events(flow, k, both)
-
-            @pl.when(now & (k == 4))
-            def _():
-                ring_events(flow, 4, tuple(way for way in both if HOPS[way][flow] == 4))
-
-    def weights_across(i):
-        @pl.when(i == 1)
-        def _():
-            x_events(0, (1,))
-
-        @pl.when((i % 2 == 1) & (i >= 3) & (i <= 7))
-        def _():
-            x_events((i - 1) // 2, (1, -1))
+    def weights(flow, k):
+        ring_events(flow, k, tuple(way for way in (1, -1) if k <= HOPS[way][flow]))
+
+    def weights_across(k):
+        x_events(k, (1, -1) if 0 < k < 4 else (1,))
 
     def adam(t):
         at = pl.ds(pl.multiple_of(t * QUARTER, QUARTER), QUARTER)
@@ -327,54 +329,79 @@
 
         lax.fori_loop(first, last, step, 0)
 
-    def step(i):
-        @pl.when(i < Z)
-        def _():
-            combine(i)
-
-        @pl.when(i + AHEAD < Z)
-        def _():
-            multiply_own(i + AHEAD)
-            multiply(i + AHEAD)
-
-        @pl.when((i >= CROSS_LAG) & (i < CROSS_LAG + Z))
-        def _():
-            cross(i - CROSS_LAG)
-
-        @pl.when(i >= TRAVEL_LAG)
-        def _():
-            travel(i - TRAVEL_LAG)
-
-        @pl.when((i >= WEIGHT_LAG) & (i <= WEIGHT_LAG + Z))
-        def _():
-            weights(i - WEIGHT_LAG)
-            weights_across(i - WEIGHT_LAG)
-
-        @pl.when(i < Z)
-        def _():
-            adam(i)
-
-        @pl.when(i == 4)
-        def _():
-            product(0)
-
-        @pl.when((i == 6) | (i == 7))
-        def _():
-            product(i - 5)
-
-    loop(0, AHEAD, multiply_own)
+    loop(0, 3, multiply_own)
     pair_g.wait_recv()
     turned_g(1)
-    loop(0, AHEAD, multiply)
+    for t in range(3):
+        multiply(t)
+    next_cot.start()
+    for t in range(EARLY, min(EARLY + 1, Z)):
+        cross_early(t)
     await_bytes(one.at[8], key_buf)
     own_w.wait()
     arrive(ACROSS, 0, 1)
     for way in (1, -1):
         ring_send(1, way, 0)
     pair_send(z, 1 - x, 0)
+    for t in range(EARLY + 1, Z):
+        cross_early(t)
+
+    def start_y(t):
+        if t < EARLY:
+            multiply_own(t)
+            multiply(t)
+        else:
+            send_first(t)
+
+    combine(0)
+    start_y(3)
+    weights(0, 1)
+    weights(2, 1)
+    loop(0, 4, adam)
+    combine(1)
+    start_y(4)
+    weights_across(0)
+    next_cot.wait_recv()
+    far_cot.start()
+    combine(2)
+    start_y(5)
+    cross(0)
+    weights(1, 1)
+    loop(4, Z, adam)
+    combine(3)
+    start_y(6)
+    cross(1)
+    weights(0, 2)
+    weights(2, 2)
+    combine(4)
+    start_y(7)
+    cross(2)
+    travel(0)
+    weights_across(1)
     own_cot.wait()
-    pair_cot.wait_recv()
-    loop(0, TRAVEL_LAG + Z, step)
+    far_cot.wait_recv()
+    product(0)
+    combine(5)
+    cross(3)
+    travel(1)
+    weights(1, 2)
+    combine(6)
+    cross(4)
+    travel(2)
+    weights(0, 3)
+    weights(2, 3)
+    product(1)
+    combine(7)
+    cross(5)
+    travel(3)
+    cross(6)
+    travel(4)
+    cross(7)
+    travel(5)
+    travel(6)
+    weights(1, 3)
+    weights_across(2)
+    travel(7)
 
     def send_fin(at, send, recv, device):
         remote(fin.at[at], fin.at[at], sent.at[send], recv, device).start()
@@ -383,20 +410,30 @@
     for r in (2, 1, 3):
         send_fin(core * 4 + y, 12, f_recv.at[r], to_y(r))
     send_fin(core * 4 + y, 14, f_recv.at[0], to_pair)
-    x_events(4, (1,))
-    loop(3, Z, product)
+    product(2)
+    weights_across(3)
+    loop(3, 5, product)
+    weights(0, 4)
+    weights(2, 4)
+    weights(1, 4)
+    loop(5, 7, product)
     for r in (1, 3, 2):
         await_bytes(f_recv.at[r], units(65))
         send_fin(core * 4 + ring(y - r, Y), 14, f_recv.at[0], to_pair)
-
-    pair_cot.wait_send()
+    weights_across(4)
+    product(7)
+
+    next_cot.wait_send()
+    far_cot.wait_send()
     pair_g.wait_send()
     await_bytes(sent.at[0], a_par)
     await_bytes(sent.at[1], w.at[pl.ds(0, 14 * SPLIT + 7 * (HALF - SPLIT))])
     await_bytes(sent.at[2], w.at[pl.ds(0, SPLIT + Z * (HALF - SPLIT))])
     await_bytes(sent.at[3], w.at[pl.ds(0, (2 * Z - 1) * HALF)])
-    for i, ref in enumerate((m1s, m1ss, m2s, m2ss, xs, xss, zs.at[pl.ds(0, Z - 1)], zss)):
+    for i, ref in enumerate((m1s, m1ss, m2s, m2ss, es, ess, zs.at[pl.ds(0, Z - 1)], zss)):
         await_bytes(sent.at[4 + i], ref)
+    for i, ref in enumerate((n1s, n1ss, n2s, n2ss, xs, xss)):
+        await_bytes(sent.at[16 + i], ref)
     for i, ref in enumerate((fin.at[pl.ds(0, 3)], fin_scale.at[pl.ds(0, 3)], fin.at[pl.ds(0, 4)], fin_scale.at[pl.ds(0, 4)])):
         await_bytes(sent.at[12 + i], ref)
     await_bytes(f_recv.at[0], units(260))
@@ -423,22 +460,29 @@
         scratch_shapes=[
             pltpu.VMEM((FEAT, COLS), BF16),
             pltpu.VMEM((TOK, COLS), BF16),
+            pltpu.VMEM((TOK, COLS // 2), BF16),
             pltpu.VMEM((4, 1024, 256), F32),
             pltpu.VMEM((Z, TOK, 2 * HALF), BF16),
             pltpu.VMEM((Z, TOK, 2 * HALF), BF16),
             pltpu.VMEM((2, TOK, COLS), BF16),
             pltpu.VMEM((COLS, 2 * TOK), BF16),
             pltpu.VMEM((Z, COLS, 2 * HALF), F32),
-            *[pltpu.VMEM((Z, 2, QUARTER, 2 * HALF), I16)] * 2,
-            *[pltpu.VMEM((Z, 2, 1, 2 * HALF), F32)] * 2,
-            *[pltpu.VMEM((Z, 2, QUARTER // 2, 2 * HALF), I16)] * 2,
-            *[pltpu.VMEM((Z, 2, 1, 2 * HALF), F32)] * 2,
+            *[pltpu.VMEM((EARLY, 2, QUARTER, 2 * HALF), I16)] * 2,
+            *[pltpu.VMEM((EARLY, 2, 1, 2 * HALF), F32)] * 2,
+            *[pltpu.VMEM((EARLY, 2, QUARTER // 2, 2 * HALF), I16)] * 2,
+            *[pltpu.VMEM((EARLY, 2, 1, 2 * HALF), F32)] * 2,
+            *[pltpu.VMEM((EARLY, QUARTER, HALF), I16)] * 2,
+            *[pltpu.VMEM((EARLY, 1, HALF), F32)] * 2,
             *[pltpu.VMEM((Z, QUARTER, HALF), I16)] * 2,
             *[pltpu.VMEM((Z, 1, HALF), F32)] * 2,
-            *[pltpu.VMEM((Z, QUARTER, HALF), I16)] * 2,
-            *[pltpu.VMEM((Z, 1, HALF), F32)] * 2,
+            *[pltpu.VMEM((Z - EARLY, 2, QUARTER, HALF), I16)] * 2,
+            *[pltpu.VMEM((Z - EARLY, 2, 1, HALF), F32)] * 2,
+            *[pltpu.VMEM((Z - EARLY, 2, QUARTER // 2, HALF), I16)] * 2,
+            *[pltpu.VMEM((Z - EARLY, 2, 1, HALF), F32)] * 2,
+            *[pltpu.VMEM((Z - EARLY, COLS, HALF), I16)] * 2,
+            *[pltpu.VMEM((Z - EARLY, Y, 1, HALF), F32)] * 2,
             pltpu.VMEM((260, 1, HALF), F32),
-            dma((9,)), dma((Z,)), dma((18,)), dma((Z,)), dma((16,)),
+            dma((11,)), dma((Z,)), dma((18,)), dma((Z,)), dma((22,)),
             dma((Z,)), dma((Z,)), dma((Z,)), dma((Z,)), dma((Y,)),
         ],
         compiler_params=pltpu.CompilerParams(

time: 67.8 us -> 65.7 us (0.969)
  Pallas kernels: 66.4 us -> 64.3 us
    pallas_call x1, Pallas kernels: 63.1 us -> 60.9 us  [gathered(): pl.pallas_call(body, out_shape=(pltpu.VMEM((TOK, FEAT), BF16), pltpu.VMEM...]
where the time goes in v4:
time: 65.7 us; the launch traced here: 65.6 us
  Pallas kernels  64.3 us (98%)
  between operations  1.29 us (2%)
    pallas_call x1, Pallas kernels, gathered(): pl.pallas_call(body, out_shape=(pltpu.VMEM((TOK, FEAT), BF16), pltpu.VMEM...  60.9 us
    pallas_call x1, Pallas kernels, written(): pl.pallas_call(write_out, out_shape=(S((2 * HALF, COLS), F32), key, key,...  3.37 us

profile of v4, /device:TPU:1, one launch (start us, length us, event | category | flops | bytes accessed | tf_op | source)
XLA Modules:
  0.0 65.6 jit_solution(1985350660560173691)
XLA Ops:
  1.3 60.9 %shard_map.128 = (bf16[256,8192]{1,0:T(8,128)(2,1)S(1)}, f32[3,1024,256]{2,1,0:T(8,128)S(1)}, s16[8,128,256]{2,1,0:T(8,128)(2,1)S(1)}, f32[8,1,256]{2,1,0:T(1,128)S(1)}) custom-call(s32[1]{0:T(128)S(6)} %copy.14.steps, bf16[256,8192]{1,0:T(8,128)(2,1)} %acts.1, bf16[256,512]{1,0:T(8,128)(2,1)} %g.1, bf16[512,512]{1,0:T(8,128)(2,1)} %pv.1, ...), custom_call_target="tpu_custom_call" | custom-call | tf_op jit(solution)/shard_map/pallas_call | solution.py:450
  62.2 3.4 %shard_map.129 = (f32[512,512]{1,0:T(8,128)}, f32[1024,256]{1,0:T(8,128)}, f32[1024,256]{1,0:T(8,128)}, f32[1024,256]{1,0:T(8,128)}, bf16[256,8192]{1,0:T(8,128)(2,1)}) custom-call(bf16[256,8192]{1,0:T(8,128)(2,1)S(1)} %get-tuple-element.9.input_grad, f32[3,1024,256]{2,1,0:T(8,128)S(1)} %get-tuple-element.10.key_out, ...), custom_call_target="tpu_custom_call" | custom-call | tf_op jit(solution)/shard_map/pallas_call | solution.py:518

commit v5 on v4

--- a/solution.py
+++ b/solution.py
@@ -381,15 +381,15 @@
     own_cot.wait()
     far_cot.wait_recv()
     product(0)
+    weights(1, 2)
     combine(5)
     cross(3)
     travel(1)
-    weights(1, 2)
     combine(6)
+    weights(0, 3)
+    weights(2, 3)
     cross(4)
     travel(2)
-    weights(0, 3)
-    weights(2, 3)
     product(1)
     combine(7)
     cross(5)
@@ -397,9 +397,9 @@
     cross(6)
     travel(4)
     cross(7)
+    weights(1, 3)
     travel(5)
     travel(6)
-    weights(1, 3)
     weights_across(2)
     travel(7)
 

time: 65.7 us -> 65.3 us (level)
  no operation moved by 1% of the time
where the time goes in v5:
time: 65.3 us; the launch traced here: 65.2 us
  Pallas kernels  63.9 us (98%)
  between operations  1.29 us (2%)
    pallas_call x1, Pallas kernels, gathered(): pl.pallas_call(body, out_shape=(pltpu.VMEM((TOK, FEAT), BF16), pltpu.VMEM...  60.5 us
    pallas_call x1, Pallas kernels, written(): pl.pallas_call(write_out, out_shape=(S((2 * HALF, COLS), F32), key, key,...  3.37 us

profile of v5, /device:TPU:1, one launch (start us, length us, event | category | flops | bytes accessed | tf_op | source)
XLA Modules:
  0.0 65.2 jit_solution(11270581557313617342)
XLA Ops:
  1.3 60.5 %shard_map.128 = (bf16[256,8192]{1,0:T(8,128)(2,1)S(1)}, f32[3,1024,256]{2,1,0:T(8,128)S(1)}, s16[8,128,256]{2,1,0:T(8,128)(2,1)S(1)}, f32[8,1,256]{2,1,0:T(1,128)S(1)}) custom-call(s32[1]{0:T(128)S(6)} %copy.14.steps, bf16[256,8192]{1,0:T(8,128)(2,1)} %acts.1, bf16[256,512]{1,0:T(8,128)(2,1)} %g.1, bf16[512,512]{1,0:T(8,128)(2,1)} %pv.1, ...), custom_call_target="tpu_custom_call" | custom-call | tf_op jit(solution)/shard_map/pallas_call | solution.py:450
  61.8 3.4 %shard_map.129 = (f32[512,512]{1,0:T(8,128)}, f32[1024,256]{1,0:T(8,128)}, f32[1024,256]{1,0:T(8,128)}, f32[1024,256]{1,0:T(8,128)}, bf16[256,8192]{1,0:T(8,128)(2,1)}) custom-call(bf16[256,8192]{1,0:T(8,128)(2,1)S(1)} %get-tuple-element.9.input_grad, f32[3,1024,256]{2,1,0:T(8,128)S(1)} %get-tuple-element.10.key_out, ...), custom_call_target="tpu_custom_call" | custom-call | tf_op jit(solution)/shard_map/pallas_call | solution.py:518
